TPU v7x, 32 devices: a whole 2x2x4 slice. The times are simulated.
32 devices in a mesh: section: 4 (over y, core), seq: 8 (over z, x).
Axes of the slice: x: 2, y: 2, z: 4, core: 2. Of those that a mesh axis runs over, the one named last changes fastest.
Arguments:
- queries: bfloat16 [4, 2, 1024, 4096], P('section', None, 'seq'), may hold values from -20 to 20
- keys_values: bfloat16 [4, 2, 1024, 8, 256], P('section', None, 'seq'), may hold values from -20 to 20
- lengths: int32 [4, 2, 4], P('section'), may hold values from 1 to 512, 1024 in all within a row
- order: int32 [4, 2], P('section'), may hold values from 0 to 1, each once within a row
Outputs:
- handoff: bfloat16 [4, 2, 1024, 4096], P('section', None, 'seq')
Inputs may be any that keep to these rules, and one draw needn't show every extreme that they name: Each row holds the lengths of 4 documents packed end to end, summing to 1024, the longest exactly 512. `order`: each row is a permutation of the microbatch numbers.
All inputs are finite; a program needn't handle non-finite values.
Results may differ from a plain program's by a relative error of at most 0.0037.
Values may be sent and summed in bfloat16 or wider, within the bound.
A program may use at most 64 MiB of HBM per device.

v0:
```python
import jax
import jax.numpy as jnp
from jax import lax
from jax.sharding import PartitionSpec as P

HD = 128
QH = 32
KVH = 8


def shortened(value):
    return jax.tree.map(lambda a: a.astype(jnp.bfloat16) if a.dtype == jnp.float32 else a, value)


def passed_along(block, axis, distance):
    devices = range(lax.axis_size(axis))
    route = [((i - distance) % len(devices), i) for i in devices]
    return lax.ppermute(block, axis, route)


def segment_ids(lengths_row, rows_all):
    ends = jnp.cumsum(lengths_row)
    position = jnp.arange(rows_all, dtype=jnp.int32)
    return jnp.sum((position[:, None] >= ends[None, :]).astype(jnp.int32), axis=1)


def attend(query_rows, pair_rows, lengths_row):
    rows_all = query_rows.shape[0]
    head_count = query_rows.shape[1] // HD
    pair_count = pair_rows.shape[1] // (2 * HD)
    share_count = head_count // pair_count
    scaling = HD ** (-0.5)
    segment = segment_ids(lengths_row, rows_all)
    position = jnp.arange(rows_all, dtype=jnp.int32)
    block_rows = min(512, rows_all)

    def one_block(block_index):
        row_start = block_index * block_rows
        query_block = lax.dynamic_slice_in_dim(query_rows, row_start, block_rows, 0)
        segment_query = lax.dynamic_slice_in_dim(segment, row_start, block_rows, 0)
        position_query = lax.dynamic_slice_in_dim(position, row_start, block_rows, 0)
        allowed = (segment_query[:, None] == segment[None, :]) & (
            position[None, :] <= position_query[:, None]
        )
        results = []
        for head_index in range(head_count):
            pair_head = head_index // share_count
            query_cols = query_block[:, head_index * HD : (head_index + 1) * HD]
            key_cols = pair_rows[:, pair_head * 2 * HD : pair_head * 2 * HD + HD]
            value_cols = pair_rows[:, pair_head * 2 * HD + HD : (pair_head + 1) * 2 * HD]
            scores = (
                lax.dot_general(
                    query_cols,
                    key_cols,
                    (((1,), (1,)), ((), ())),
                    preferred_element_type=jnp.float32,
                )
                * scaling
            )
            peaks = jnp.max(jnp.where(allowed, scores, -jnp.inf), axis=1, keepdims=True)
            weights = jnp.where(allowed, jnp.exp(scores - peaks), jnp.float32(0.0))
            totals = jnp.sum(weights, axis=1, keepdims=True)
            mixed = (
                jnp.dot(
                    weights.astype(jnp.bfloat16), value_cols, preferred_element_type=jnp.float32
                )
                / totals
            )
            results.append(mixed.astype(jnp.bfloat16))
        return jnp.concatenate(results, axis=1)

    blocks = lax.map(one_block, jnp.arange(rows_all // block_rows, dtype=jnp.int32))
    return blocks.reshape(rows_all, head_count * HD)


def reorder(stacked, order_row):
    picked_all = []
    for slot in range(stacked.shape[0]):
        picked = stacked[0]
        picked = jnp.where(order_row[slot] == 1, stacked[1], picked)
        picked_all.append(picked)
    return jnp.stack(picked_all, axis=0)


def local(queries, keys_values, lengths, order):
    n_seq = lax.axis_size("seq")
    micro = queries.shape[1]
    tok_rows = queries.shape[2]
    all_rows = tok_rows * n_seq
    per_device = QH // n_seq
    repeat_count = max(1, n_seq // KVH)
    kv_local = max(1, KVH // n_seq)
    query_split = queries.reshape(micro, tok_rows, n_seq, per_device * HD)
    wide = jnp.repeat(keys_values.reshape(micro, tok_rows, KVH, 2 * HD), repeat_count, axis=2)
    head_queries, head_pairs = (
        lax.all_to_all(query_split, "seq", split_axis=2, concat_axis=1, tiled=True),
        lax.all_to_all(wide, "seq", split_axis=2, concat_axis=1, tiled=True),
    )
    head_queries = head_queries.reshape(micro, all_rows, per_device * HD)
    head_pairs = head_pairs.reshape(micro, all_rows, kv_local * 2 * HD)
    contexts = jnp.stack(
        [
            attend(head_queries[index_mb], head_pairs[index_mb], lengths[0, index_mb])
            for index_mb in range(micro)
        ],
        axis=0,
    )
    contexts = contexts.reshape(micro, all_rows, 1, per_device * HD)
    sent = passed_along(shortened(reorder(contexts, order[0])), "section", 1)
    result = lax.all_to_all(shortened(sent), "seq", split_axis=1, concat_axis=2, tiled=True).astype(
        sent.dtype
    )
    return result.reshape(1, micro, tok_rows, QH * HD)


def solution(mesh):
    placed = (
        P("section", None, "seq", None),
        P("section", None, "seq", None, None),
        P("section", None, None),
        P("section", None),
    )
    return jax.shard_map(
        local,
        mesh=mesh,
        in_specs=placed,
        out_specs=P("section", None, "seq", None),
        check_vma=False,
    )
```

profile of v0, /device:TPU:24, one launch (start us, length us, event | category | flops | bytes accessed | tf_op | source)
XLA Modules:
  0.0 259.1 jit_solution(17375351473633446763)
XLA Ops:
  0.0 2.5 copy.71
  2.5 6.0 %all-to-all-start.1 = ((bf16[2,128,8,256]{3,1,0,2:T(8,128)(2,1)}), bf16[2,128,8,256]{3,1,0,2:T(8,128)(2,1)}, u32[]{:S(2)}, u32[]{:S(2)}) async-start(bf16[2,128,8,256]{3,1,0,2:T(8,128)(2,1)} %bitcast.33), calls=%async_computation.1 | async-start | bytes 2097152 | tf_op jit(solution)/shard_map/all_to_all | solution.py:97
  8.5 3.1 %copy.55 = bf16[1,2,128,4096]{2,3,1,0:T(8,128)(2,1)S(1)} copy(bf16[1,2,128,4096]{3,2,1,0:T(8,128)(2,1)} %param.8) | data formatting | bytes 4194304 | tf_op args[0]
  11.7 2.6 %copy.56 = bf16[2,128,8,512]{3,1,0,2:T(8,128)(2,1)} copy(bf16[2,128,8,512]{1,3,2,0:T(8,128)(2,1)S(1)} %bitcast.47) | data formatting | bytes 4194304 | tf_op jit(solution)/shard_map/reshape | solution.py:93
  14.3 17.4 %all-to-all-done.1 = bf16[2,128,8,256]{3,1,0,2:T(8,128)(2,1)} async-done(((bf16[2,128,8,256]{3,1,0,2:T(8,128)(2,1)}), bf16[2,128,8,256]{3,1,0,2:T(8,128)(2,1)}, u32[]{:S(2)}, u32[]{:S(2)}) %all-to-all-start.1) | async-done | bytes 1048608 | tf_op jit(solution)/shard_map/all_to_all | solution.py:97
  31.7 6.3 %all-to-all-start = ((bf16[2,128,8,512]{3,1,0,2:T(8,128)(2,1)}), bf16[2,128,8,512]{3,1,0,2:T(8,128)(2,1)S(1)}, u32[]{:S(2)}, u32[]{:S(2)}) async-start(bf16[2,128,8,512]{3,1,0,2:T(8,128)(2,1)} %copy.56), calls=%async_computation | async-start | bytes 4194304 | tf_op jit(solution)/shard_map/all_to_all | solution.py:96
  40.5 1.3 fusion.87
  41.8 43.0 %all-to-all-done = bf16[2,128,8,512]{3,1,0,2:T(8,128)(2,1)S(1)} async-done(((bf16[2,128,8,512]{3,1,0,2:T(8,128)(2,1)}), bf16[2,128,8,512]{3,1,0,2:T(8,128)(2,1)S(1)}, u32[]{:S(2)}, u32[]{:S(2)}) %all-to-all-start) | async-done | bytes 2097184 | tf_op jit(solution)/shard_map/all_to_all | solution.py:96
  84.9 1.5 fusion.86
  86.4 1.0 broadcast.55.clone2
  87.4 42.2 %while.22 = (s32[]{:T(128)}, bf16[2,512,512]{2,1,0:T(8,128)(2,1)}, s32[2]{0:T(128)S(1)}, s32[1024]{0:T(1024)S(1)}, s32[1024]{0:T(1024)S(1)}, /*index=5*/bf16[102...) while((s32[]{:T(128)}, bf16[2,512,512]{2,1,0:T(8,128)(2,1)}, ...), condition=%wide.region_11.12_spmd.clone, body=%wide.region_2.11_spmd.clone.sunk | while | flops 1110437888 | bytes 60952956 | solution.py:72
  88.8 2.7 %select_reduce_fusion.10 = (f32[512]{0:T(512)S(1)}, f32[512,1024]{1,0:T(8,128)}) fusion(s32[512]{0:T(512)S(1)} %dynamic_slice.40, s32[1024]{0:T(1024)S(1)} %get-tuple-element.339, s32[1024]{0:T(1024)S(1)} %get-tuple-element.338, s32[512]{0:T(512)S(1)} %dynamic_slice.41, bf16[1024,256]{1,0:T(8,128)(2,1)S(1)} %get-tuple-element.341, ...), kind=kOutput, calls=%fused_computation.7.clone.1 | convolution fusion | flops 137362944 | bytes 2504708 | tf_op jit(solution)/shard_map/while/body/eval_jaxpr/dot_general | solution.py:52
  91.5 1.3 fusion.141
  92.9 2.7 %fusion.142 = f32[512,1024]{1,0:T(8,128)} fusion(bf16[1024,256]{1,0:T(8,128)(2,1)S(1)} %get-tuple-element.341, bf16[1024,512]{1,0:T(8,128)(2,1)} %get-tuple-element.340, s32[]{:T(128)S(6)} %select_n.205, s32[]{:T(128)S(6)} %add.39), kind=kOutput, calls=%fused_computation.34.clone.1 | convolution fusion | flops 134217728 | bytes 2490376 | tf_op jit(solution)/shard_map/while/body/eval_jaxpr/dot_general | solution.py:52
  95.6 4.2 %fusion.143 = (f32[512]{0:T(512)S(1)}, f32[512]{0:T(512)S(1)}, f32[512]{0:T(512)S(1)}, f32[512]{0:T(512)S(1)}, f32[512,1024]{1,0:T(8,128)S(1)}) fusion(f32[512,1024]{1,0:T(8,128)} %get-tuple-element.280, f32[512]{0:T(512)S(1)} %get-tuple-element.281, s32[512]{0:T(512)S(1)} %dynamic_slice.40, s32[1024]{0:T(1024)S(1)} %get-tuple-element.339, ...), kind=kOutput, calls=%fused_computation.9.clone.1 | convolution fusion | flops 142604288 | bytes 8804360 | tf_op jit(solution)/shard_map/while/body/eval_jaxpr/dot_general | solution.py:52
  101.4 2.2 fusion.144
  103.6 0.9 fusion.147
  106.5 1.0 copy-done.4
  107.5 1.0 copy-done.5
  109.9 2.8 %select_reduce_fusion.10 = (f32[512]{0:T(512)S(1)}, f32[512,1024]{1,0:T(8,128)}) fusion(s32[512]{0:T(512)S(1)} %dynamic_slice.40, s32[1024]{0:T(1024)S(1)} %get-tuple-element.339, s32[1024]{0:T(1024)S(1)} %get-tuple-element.338, s32[512]{0:T(512)S(1)} %dynamic_slice.41, bf16[1024,256]{1,0:T(8,128)(2,1)S(1)} %get-tuple-element.341, ...), kind=kOutput, calls=%fused_computation.7.clone.1 | convolution fusion | flops 137362944 | bytes 2504708 | tf_op jit(solution)/shard_map/while/body/eval_jaxpr/dot_general | solution.py:52
  112.7 1.3 fusion.141
  114.0 2.7 %fusion.142 = f32[512,1024]{1,0:T(8,128)} fusion(bf16[1024,256]{1,0:T(8,128)(2,1)S(1)} %get-tuple-element.341, bf16[1024,512]{1,0:T(8,128)(2,1)} %get-tuple-element.340, s32[]{:T(128)S(6)} %select_n.205, s32[]{:T(128)S(6)} %add.39), kind=kOutput, calls=%fused_computation.34.clone.1 | convolution fusion | flops 134217728 | bytes 2490376 | tf_op jit(solution)/shard_map/while/body/eval_jaxpr/dot_general | solution.py:52
  116.7 4.2 %fusion.143 = (f32[512]{0:T(512)S(1)}, f32[512]{0:T(512)S(1)}, f32[512]{0:T(512)S(1)}, f32[512]{0:T(512)S(1)}, f32[512,1024]{1,0:T(8,128)S(1)}) fusion(f32[512,1024]{1,0:T(8,128)} %get-tuple-element.280, f32[512]{0:T(512)S(1)} %get-tuple-element.281, s32[512]{0:T(512)S(1)} %dynamic_slice.40, s32[1024]{0:T(1024)S(1)} %get-tuple-element.339, ...), kind=kOutput, calls=%fused_computation.9.clone.1 | convolution fusion | flops 142604288 | bytes 8804360 | tf_op jit(solution)/shard_map/while/body/eval_jaxpr/dot_general | solution.py:52
  122.5 2.2 fusion.144
  127.7 1.0 copy-done.4
  128.7 1.0 copy-done.5
  129.6 1.1 broadcast.55.clone2.1
  130.7 42.1 %while.23 = (s32[]{:T(128)}, bf16[2,512,512]{2,1,0:T(8,128)(2,1)}, s32[2]{0:T(128)S(1)}, s32[1024]{0:T(1024)S(1)}, s32[1024]{0:T(1024)S(1)}, /*index=5*/bf16[102...) while((s32[]{:T(128)}, bf16[2,512,512]{2,1,0:T(8,128)(2,1)}, ...), condition=%wide.region_23.24_spmd.clone, body=%wide.region_14.23_spmd.clone.sunk | while | flops 1110437888 | bytes 60952956 | solution.py:72
  132.1 2.8 %select_reduce_fusion.11 = (f32[512]{0:T(512)S(1)}, f32[512,1024]{1,0:T(8,128)}) fusion(s32[512]{0:T(512)S(1)} %dynamic_slice.43, s32[1024]{0:T(1024)S(1)} %get-tuple-element.381, s32[1024]{0:T(1024)S(1)} %get-tuple-element.380, s32[512]{0:T(512)S(1)} %dynamic_slice.44, bf16[1024,256]{1,0:T(8,128)(2,1)S(1)} %get-tuple-element.383, ...), kind=kOutput, calls=%fused_computation.61.clone.1 | convolution fusion | flops 137362944 | bytes 2504708 | tf_op jit(solution)/shard_map/while/body/eval_jaxpr/dot_general | solution.py:52
  134.8 1.3 fusion.161
  136.2 2.7 %fusion.162 = f32[512,1024]{1,0:T(8,128)} fusion(bf16[1024,256]{1,0:T(8,128)(2,1)S(1)} %get-tuple-element.383, bf16[1024,512]{1,0:T(8,128)(2,1)} %get-tuple-element.382, s32[]{:T(128)S(6)} %select_n.213, s32[]{:T(128)S(6)} %add.44), kind=kOutput, calls=%fused_computation.88.clone.1 | convolution fusion | flops 134217728 | bytes 2490376 | tf_op jit(solution)/shard_map/while/body/eval_jaxpr/dot_general | solution.py:52
  138.9 4.2 %fusion.163 = (f32[512]{0:T(512)S(1)}, f32[512]{0:T(512)S(1)}, f32[512]{0:T(512)S(1)}, f32[512]{0:T(512)S(1)}, f32[512,1024]{1,0:T(8,128)S(1)}) fusion(f32[512,1024]{1,0:T(8,128)} %get-tuple-element.297, f32[512]{0:T(512)S(1)} %get-tuple-element.298, s32[512]{0:T(512)S(1)} %dynamic_slice.43, s32[1024]{0:T(1024)S(1)} %get-tuple-element.381, ...), kind=kOutput, calls=%fused_computation.63.clone.1 | convolution fusion | flops 142604288 | bytes 8804360 | tf_op jit(solution)/shard_map/while/body/eval_jaxpr/dot_general | solution.py:52
  144.7 2.2 fusion.164
  149.8 1.0 copy-done.2
  150.8 1.0 copy-done.3
  153.2 2.7 %select_reduce_fusion.11 = (f32[512]{0:T(512)S(1)}, f32[512,1024]{1,0:T(8,128)}) fusion(s32[512]{0:T(512)S(1)} %dynamic_slice.43, s32[1024]{0:T(1024)S(1)} %get-tuple-element.381, s32[1024]{0:T(1024)S(1)} %get-tuple-element.380, s32[512]{0:T(512)S(1)} %dynamic_slice.44, bf16[1024,256]{1,0:T(8,128)(2,1)S(1)} %get-tuple-element.383, ...), kind=kOutput, calls=%fused_computation.61.clone.1 | convolution fusion | flops 137362944 | bytes 2504708 | tf_op jit(solution)/shard_map/while/body/eval_jaxpr/dot_general | solution.py:52
  155.9 1.3 fusion.161
  157.2 2.7 %fusion.162 = f32[512,1024]{1,0:T(8,128)} fusion(bf16[1024,256]{1,0:T(8,128)(2,1)S(1)} %get-tuple-element.383, bf16[1024,512]{1,0:T(8,128)(2,1)} %get-tuple-element.382, s32[]{:T(128)S(6)} %select_n.213, s32[]{:T(128)S(6)} %add.44), kind=kOutput, calls=%fused_computation.88.clone.1 | convolution fusion | flops 134217728 | bytes 2490376 | tf_op jit(solution)/shard_map/while/body/eval_jaxpr/dot_general | solution.py:52
  159.9 4.2 %fusion.163 = (f32[512]{0:T(512)S(1)}, f32[512]{0:T(512)S(1)}, f32[512]{0:T(512)S(1)}, f32[512]{0:T(512)S(1)}, f32[512,1024]{1,0:T(8,128)S(1)}) fusion(f32[512,1024]{1,0:T(8,128)} %get-tuple-element.297, f32[512]{0:T(512)S(1)} %get-tuple-element.298, s32[512]{0:T(512)S(1)} %dynamic_slice.43, s32[1024]{0:T(1024)S(1)} %get-tuple-element.381, ...), kind=kOutput, calls=%fused_computation.63.clone.1 | convolution fusion | flops 142604288 | bytes 8804360 | tf_op jit(solution)/shard_map/while/body/eval_jaxpr/dot_general | solution.py:52
  165.7 2.2 fusion.164
  170.9 1.0 copy-done.2
  171.9 1.0 copy-done.3
  172.8 1.7 broadcast_select_fusion.1
  174.8 25.4 %collective-permute-done = bf16[2,1024,1,512]{3,1,2,0:T(8,128)(2,1)S(1)} collective-permute-done((bf16[2,1024,1,512]{3,1,2,0:T(8,128)(2,1)S(1)}, bf16[2,1024,1,512]{3,1,2,0:T(8,128)(2,1)S(1)}, u32[]{:S(2)}, u32[]{:S(2)}) %collective-permute-start) | collective-permute-done | bytes 2097184 | tf_op jit(solution)/shard_map/ppermute | solution.py:18
  200.2 2.2 copy.62
  202.4 49.9 %all_to_all.45 = bf16[2,1024,1,512]{3,0,2,1:T(2,128)(2,1)S(1)} all-to-all(bf16[2,1024,1,512]{3,0,2,1:T(2,128)(2,1)S(1)} %copy.62), channel_id=1, replica_groups=mesh['section'=4,'seq'=8] {'seq'}, dimensions={1} | all-to-all | bytes 4194304 | tf_op jit(solution)/shard_map/all_to_all | solution.py:110
  252.6 2.4 copy.64
  255.0 4.1 %copy.65 = bf16[1,2,128,4096]{3,2,1,0:T(8,128)(2,1)} copy(bf16[1,2,128,4096]{2,3,1,0:T(8,128)(2,1)} %bitcast.46) | data formatting | bytes 4194304 | tf_op jit(solution)/shard_map/reshape | solution.py:113
  (80 shorter events, 21.9 us)
Async XLA Ops:
  2.5 29.2 %all-to-all-start.1 = ((bf16[2,128,8,256]{3,1,0,2:T(8,128)(2,1)}), bf16[2,128,8,256]{3,1,0,2:T(8,128)(2,1)}, u32[]{:S(2)}, u32[]{:S(2)}) async-start(bf16[2,128,8,256]{3,1,0,2:T(8,128)(2,1)} %bitcast.33), calls=%async_computation.1 | async-start | bytes 2097152 | tf_op jit(solution)/shard_map/all_to_all | solution.py:97
  14.3 23.7 %copy-start.7 = (s32[1,2,4]{2,1,0:T(2,128)S(1)}, s32[1,2,4]{2,1,0:T(2,128)}, u32[]{:S(2)}) copy-start(s32[1,2,4]{2,1,0:T(2,128)} %param.10) | copy-start | bytes 100
  14.3 24.1 %copy-start.6 = (s32[1,2]{1,0:T(1,128)S(1)}, s32[1,2]{1,0:T(1,128)}, u32[]{:S(2)}) copy-start(s32[1,2]{1,0:T(1,128)} %param.11) | copy-start | bytes 28
  31.7 53.1 %all-to-all-start = ((bf16[2,128,8,512]{3,1,0,2:T(8,128)(2,1)}), bf16[2,128,8,512]{3,1,0,2:T(8,128)(2,1)S(1)}, u32[]{:S(2)}, u32[]{:S(2)}) async-start(bf16[2,128,8,512]{3,1,0,2:T(8,128)(2,1)} %copy.56), calls=%async_computation | async-start | bytes 4194304 | tf_op jit(solution)/shard_map/all_to_all | solution.py:96
  95.6 4.2 %copy-start.8 = (f32[512,1024]{1,0:T(8,128)S(1)}, f32[512,1024]{1,0:T(8,128)}, u32[]{:S(2)}) copy-start(f32[512,1024]{1,0:T(8,128)} %get-tuple-element.280) | copy-start | bytes 6291460 | tf_op jit(solution)/shard_map/while
  99.8 1.6 copy-start
  106.3 1.2 copy-start.4
  107.5 1.0 copy-start.5
  116.7 4.2 %copy-start.8 = (f32[512,1024]{1,0:T(8,128)S(1)}, f32[512,1024]{1,0:T(8,128)}, u32[]{:S(2)}) copy-start(f32[512,1024]{1,0:T(8,128)} %get-tuple-element.280) | copy-start | bytes 6291460 | tf_op jit(solution)/shard_map/while
  120.9 1.6 copy-start
  127.4 1.2 copy-start.4
  128.7 1.0 copy-start.5
  138.9 4.2 %copy-start.9 = (f32[512,1024]{1,0:T(8,128)S(1)}, f32[512,1024]{1,0:T(8,128)}, u32[]{:S(2)}) copy-start(f32[512,1024]{1,0:T(8,128)} %get-tuple-element.297) | copy-start | bytes 6291460 | tf_op jit(solution)/shard_map/while
  143.1 1.6 copy-start.1
  149.5 1.2 copy-start.2
  150.8 1.0 copy-start.3
  159.9 4.2 %copy-start.9 = (f32[512,1024]{1,0:T(8,128)S(1)}, f32[512,1024]{1,0:T(8,128)}, u32[]{:S(2)}) copy-start(f32[512,1024]{1,0:T(8,128)} %get-tuple-element.297) | copy-start | bytes 6291460 | tf_op jit(solution)/shard_map/while
  164.1 1.6 copy-start.1
  170.6 1.2 copy-start.2
  171.8 1.0 copy-start.3
  174.7 25.5 %collective-permute-start = (bf16[2,1024,1,512]{3,1,2,0:T(8,128)(2,1)S(1)}, bf16[2,1024,1,512]{3,1,2,0:T(8,128)(2,1)S(1)}, u32[]{:S(2)}, u32[]{:S(2)}) collective-permute-start(bf16[2,1024,1,512]{3,1,2,0:T(8,128)(2,1)S(1)} %pad_maximum_fusion), channel_id=1, source_target_pairs={{24,0},{0,8},{8,16},{16,24},{25,1},{1,9},{9,17},{17,25},{26,2},{2,... | collective-permute-start | bytes 6291464 | tf_op jit(solution)/shard_map/ppermute | solution.py:18
where the time goes:
time: 264 us; the launch traced here: 259 us
  waiting for transfers between devices  85.9 us (33%)
  matrix products  58 us (22%)
  blocking collectives  49.9 us (19%)
  local copies, waits for them, and re-layouts  37.1 us (14%)
  starting transfers between devices  12.4 us (5%)
  other arithmetic  11.4 us (4%)
  loops' own time  2.97 us (1%)
    all_to_all x1, blocking collectives, local(): lax.all_to_all(shortened(sent), 'seq', split_axis=1, concat_axis=2, tiled...  49.9 us
    dot_general x16, matrix products, one_block(): lax.dot_general(query_cols, key_cols, (((1,), (1,)), ((), ())), preferred...  43.8 us
    all_to_all x1, waiting for transfers between devices, local(): lax.all_to_all(query_split, 'seq', split_axis=2, concat_axis=1, tiled=True)  43 us
    ppermute x1, waiting for transfers between devices, passed_along(): return lax.ppermute(block, axis, route)  25.4 us
    all_to_all x1, waiting for transfers between devices, local(): lax.all_to_all(wide, 'seq', split_axis=2, concat_axis=1, tiled=True)  17.4 us
    dot_general x16, matrix products, one_block(): jnp.dot(weights.astype(jnp.bfloat16), value_cols, preferred_element_type=...  14.2 us
    while x32, local copies, waits for them, and re-layouts  10.4 us
    reduce_sum x4, other arithmetic, one_block(): totals = jnp.sum(weights, axis=1, keepdims=True)  8.87 us
  transfers between devices with their start and end apart: 3, of which 3 were waited for; matrix products, arithmetic and copies ran while one was open for 3% of the time, Pallas kernels for 0%

commit v1 on v0

v1 whole, which is shorter than its diff:
```python
import math

import jax
import jax.numpy as jnp
from jax import lax
from jax.experimental import pallas as pl
from jax.experimental.pallas import tpu as pltpu
from jax.sharding import PartitionSpec as P

MESH = pl.DeviceIdType.MESH
LEAD = 3
MASKED = -1e30


def row_width(count):
    return max(w for w in range(1, count + 1) if count % w == 0 and w * w <= count)


def kernel(
    lengths_ref,
    order_ref,
    q_hbm,
    kv_hbm,
    out_hbm,
    kvbuf,
    qbuf,
    obuf,
    bias,
    local_sem,
    recv_sem,
    column_sem,
    row_sem,
    osend_sem,
    orecv_sem,
):
    n = lax.axis_size("seq")
    sections = lax.axis_size("section")
    width = row_width(n)
    depth = n // width
    reach = n // 2
    hops = -(-reach // width)
    micro, tok, q_cols = qbuf.shape
    chunks, keys, pair = kvbuf.shape
    head = pair // 2
    groups = chunks // micro
    out_cols = q_cols // groups
    share = out_cols // head
    docs = lengths_ref.shape[2]

    me = lax.axis_index("seq")
    section = lax.axis_index("section")
    x = me % width
    z = me // width
    row_moves = [
        (k, dx)
        for k in range(hops + 1)
        for dx in range(1 - width, width)
        if dx != 0 and 1 <= k * width + dx <= reach
    ]

    def slot(c, d):
        return kvbuf.at[c, pl.ds(d * tok, tok), :]

    def source(c, k):
        return kv_hbm.at[c] if k == 0 else slot(c, k * width)

    def column_copy(c, k):
        return pltpu.make_async_remote_copy(
            src_ref=source(c, k),
            dst_ref=slot(c, (k + 1) * width),
            send_sem=column_sem.at[k, c],
            recv_sem=recv_sem.at[(k + 1) * width, c],
            device_id=(section, me + width),
            device_id_type=MESH,
        )

    def row_copy(c, index):
        k, dx = row_moves[index]
        return pltpu.make_async_remote_copy(
            src_ref=source(c, k),
            dst_ref=slot(c, k * width + dx),
            send_sem=row_sem.at[index, c],
            recv_sem=recv_sem.at[k * width + dx, c],
            device_id=(section, me + dx),
            device_id_type=MESH,
        )

    def out_copy(c):
        columns = pl.ds(pl.multiple_of((c % groups) * out_cols, out_cols), out_cols)
        return pltpu.make_async_remote_copy(
            src_ref=obuf.at[c],
            dst_ref=out_hbm.at[0, c // groups, :, columns],
            send_sem=osend_sem.at[c],
            recv_sem=orecv_sem.at[c],
            device_id=((section + 1) % sections, me),
            device_id_type=MESH,
        )

    def each_send(c, k, act):
        if k < hops and (k + 1) * width <= reach:

            @pl.when((z + 1 < depth) & (z >= k))
            def _():
                act(column_copy(c, k))

        for index, (move_k, dx) in enumerate(row_moves):
            if move_k == k:

                @pl.when((x + dx >= 0) & (x + dx < width) & (z >= k))
                def _(index=index):
                    act(row_copy(c, index))

    def start_sends(c, k):
        each_send(c, k, lambda copy: copy.start())

    def arrived(c, d):
        @pl.when(me >= d)
        def _():
            pltpu.make_async_copy(slot(c, d), slot(c, d), recv_sem.at[d, c]).wait()

    barrier = pltpu.get_barrier_semaphore()

    def greet(condition, target):
        @pl.when(condition)
        def _():
            pl.semaphore_signal(barrier, inc=1, device_id=target, device_id_type=MESH)

    greet(z > 0, (section, me - width))
    greet(z + 1 < depth, (section, me + width))
    for dx in range(1 - width, width):
        if dx != 0:
            greet((x + dx >= 0) & (x + dx < width), (section, me + dx))
    for step in (1, sections - 1):
        greet(me >= 0, ((section + step) % sections, me))

    q_copy = pltpu.make_async_copy(q_hbm.at[0], qbuf, local_sem.at[0])
    kv_copy = pltpu.make_async_copy(kv_hbm, kvbuf.at[:, pl.ds(0, tok), :], local_sem.at[1])
    q_copy.start()
    kv_copy.start()

    for d in range(1, reach + 1):

        @pl.when(me < d)
        def _(d=d):
            def clear(c, carry):
                kvbuf[c, pl.ds(d * tok, tok), :] = jnp.zeros((tok, pair), kvbuf.dtype)
                return carry

            lax.fori_loop(0, chunks, clear, 0)

    for j in range(micro):
        m = order_ref[0, j]
        own = me * tok + lax.broadcasted_iota(jnp.int32, (tok, tok), 0)
        end = jnp.int32(0)
        begin = jnp.zeros((tok, tok), jnp.int32)
        for document in range(docs):
            end = end + lengths_ref[0, m, document]
            begin = jnp.where(own >= end, end, begin)
        for d in range(reach + 1):
            other = (me - d) * tok + lax.broadcasted_iota(jnp.int32, (tok, tok), 1)
            allowed = (other >= begin) & (other <= own)
            bias[j, :, pl.ds(d * tok, tok)] = jnp.where(allowed, 0.0, MASKED)

    column_mates = jnp.where(z > 0, 1, 0) + jnp.where(z + 1 < depth, 1, 0)
    pl.semaphore_wait(barrier, column_mates + (width - 1) + 2)

    lead = min(LEAD, chunks)
    for c in range(lead):
        start_sends(c, 0)
    q_copy.wait()
    kv_copy.wait()

    factor = head**-0.5 * math.log2(math.e)

    def compute(c):
        j = c // groups
        columns = pl.ds(pl.multiple_of((c % groups) * out_cols, out_cols), out_cols)
        q = qbuf[order_ref[0, j], :, columns]
        rows = jnp.concatenate([q[:, h * head : (h + 1) * head] for h in range(share)], axis=0)
        k = kvbuf[c, :, :head]
        v = kvbuf[c, :, head:]
        scores = lax.dot_general(
            rows, k, (((1,), (1,)), ((), ())), preferred_element_type=jnp.float32
        )
        hidden = bias[j]
        for h in range(share):
            part = scores[h * tok : (h + 1) * tok] * factor + hidden
            weights = jnp.exp2(part - jnp.max(part, axis=1, keepdims=True))
            totals = jnp.sum(weights, axis=1, keepdims=True)
            mixed = jnp.dot(weights.astype(jnp.bfloat16), v, preferred_element_type=jnp.float32)
            obuf[c, :, h * head : (h + 1) * head] = (mixed / totals).astype(obuf.dtype)

    def turn(t, carry):
        @pl.when(t + lead < chunks)
        def _():
            start_sends(t + lead, 0)

        for k in range(1, hops + 1):
            if k * width <= reach:

                @pl.when((t - (k - 1) >= 0) & (t - (k - 1) < chunks))
                def _(k=k):
                    arrived(t - (k - 1), k * width)
                    start_sends(t - (k - 1), k)

        @pl.when(t >= hops)
        def _():
            c = t - hops
            for d in range(1, reach + 1):
                if d % width != 0:
                    arrived(c, d)
            compute(c)
            out_copy(c).start()

        return carry

    lax.fori_loop(0, chunks + hops, turn, 0)

    def drain(c, carry):
        for k in range(hops + 1):
            each_send(c, k, lambda copy: copy.wait_send())
        out_copy(c).wait()
        return carry

    lax.fori_loop(0, chunks, drain, 0)


def local(queries, keys_values, lengths, order):
    n = lax.axis_size("seq")
    width = row_width(n)
    reach = n // 2
    hops = -(-reach // width)
    _, micro, tok, q_cols = queries.shape
    groups, pair = keys_values.shape[3:]
    chunks = micro * groups
    out_cols = q_cols // groups
    moves = sum(
        1
        for k in range(hops + 1)
        for dx in range(1 - width, width)
        if dx != 0 and 1 <= k * width + dx <= reach
    )

    picked = []
    for j in range(micro):
        one = keys_values[0, 0]
        for m in range(1, micro):
            one = jnp.where(order[0, j] == m, keys_values[0, m], one)
        picked.append(one)
    pairs = jnp.stack(picked).transpose(0, 2, 1, 3).reshape(chunks, tok, pair)

    keys = (reach + 1) * tok
    return pl.pallas_call(
        kernel,
        out_shape=jax.ShapeDtypeStruct(queries.shape, queries.dtype),
        in_specs=[
            pl.BlockSpec(memory_space=pltpu.SMEM),
            pl.BlockSpec(memory_space=pltpu.SMEM),
            pl.BlockSpec(memory_space=pl.ANY),
            pl.BlockSpec(memory_space=pl.ANY),
        ],
        out_specs=pl.BlockSpec(memory_space=pl.ANY),
        scratch_shapes=[
            pltpu.VMEM((chunks, keys, pair), jnp.bfloat16),
            pltpu.VMEM((micro, tok, q_cols), jnp.bfloat16),
            pltpu.VMEM((chunks, tok, out_cols), jnp.bfloat16),
            pltpu.VMEM((micro, tok, keys), jnp.float32),
            pltpu.SemaphoreType.DMA((2,)),
            pltpu.SemaphoreType.DMA((reach + 1, chunks)),
            pltpu.SemaphoreType.DMA((hops, chunks)),
            pltpu.SemaphoreType.DMA((max(1, moves), chunks)),
            pltpu.SemaphoreType.DMA((chunks,)),
            pltpu.SemaphoreType.DMA((chunks,)),
        ],
        compiler_params=pltpu.CompilerParams(
            collective_id=0,
            has_side_effects=True,
            vmem_limit_bytes=48 * 1024 * 1024,
        ),
        name="relay_attention",
    )(lengths, order, queries, pairs)


def solution(mesh):
    placed = (
        P("section", None, "seq", None),
        P("section", None, "seq", None, None),
        P("section", None, None),
        P("section", None),
    )
    return jax.shard_map(
        local,
        mesh=mesh,
        in_specs=placed,
        out_specs=P("section", None, "seq", None),
        check_vma=False,
    )
```

time: 264 us -> 66.9 us (0.25); the launches traced: 259 us -> 66.7 us
  waiting for transfers between devices: 85.9 us -> 0 us
  Pallas kernels: 0 us -> 60 us
  matrix products: 58 us -> 0 us
  blocking collectives: 49.9 us -> 0 us
  local copies, waits for them, and re-layouts: 37.1 us -> 4.09 us
  starting transfers between devices: 12.4 us -> 0 us
  other arithmetic: 11.4 us -> 1.37 us
  loops' own time: 2.97 us -> 0 us
    all_to_all x2 -> x0, waiting for transfers between devices: 60.5 us -> none  [the longest x1 43 us: local(): lax.all_to_all(query_split, 'seq', split_axis=2, concat_axis=1, tiled=True)]
    pallas_call x0 -> x1, Pallas kernels: none -> 60 us  [local(): pl.pallas_call(kernel, out_shape=jax.ShapeDtypeStruct(queries.shape, quer...]
    dot_general x32 -> x0, matrix products: 58 us -> none  [the longest x16 43.8 us: one_block(): lax.dot_general(query_cols, key_cols, (((1,), (1,)), ((), ())), preferred...]
    all_to_all x1 -> x0, blocking collectives: 49.9 us -> none  [local(): lax.all_to_all(shortened(sent), 'seq', split_axis=1, concat_axis=2, tiled...]
    ppermute x1 -> x0, waiting for transfers between devices: 25.4 us -> none  [passed_along(): return lax.ppermute(block, axis, route)]
    all_to_all x2 -> x0, starting transfers between devices: 12.3 us -> none  [the longest x1 6.28 us: local(): lax.all_to_all(query_split, 'seq', split_axis=2, concat_axis=1, tiled=True)]
    while x32 -> x0, local copies, waits for them, and re-layouts: 10.4 us -> none
    reduce_sum x6 -> x0, other arithmetic: 9.03 us -> none  [the longest x4 8.87 us: one_block(): totals = jnp.sum(weights, axis=1, keepdims=True)]
  transfers between devices with their start and end apart: 3 -> 0, of which waited for: 3 -> 0; matrix products, arithmetic and copies ran while one was open for 3% -> 0% of each run, Pallas kernels for 0% -> 0%
where the time goes in v1:
time: 66.9 us; the launch traced here: 66.7 us
  Pallas kernels  60 us (90%)
  local copies, waits for them, and re-layouts  4.09 us (6%)
  other arithmetic  1.37 us (2%)
  between operations  1.27 us (2%)
    pallas_call x1, Pallas kernels, local(): pl.pallas_call(kernel, out_shape=jax.ShapeDtypeStruct(queries.shape, quer...  60 us
    unnamed x7, local copies, waits for them, and re-layouts  2.56 us

profile of v1, /device:TPU:24, one launch (start us, length us, event | category | flops | bytes accessed | tf_op | source)
XLA Modules:
  0.0 66.7 jit_solution(9748973365157063114)
XLA Ops:
  0.0 1.3 %fusion = (s32[1,1]{1,0:T(1,128)}, s32[1,1]{1,0:T(1,128)}) fusion(s32[1,2]{1,0:T(1,128)} %order_ref.1), kind=kLoop, calls=%fused_computation.3 | loop fusion | bytes 16 | tf_op jit(solution)/shard_map/slice | solution.py:248
  2.5 1.3 %select_bitcast_fusion.1 = (bf16[1,128,8,256]{3,2,1,0:T(8,128)(2,1)S(1)}, bf16[1,128,8,256]{3,2,1,0:T(8,128)(2,1)S(1)}) fusion(pred[]{:T(512)} %bitcast, bf16[1,2,128,8,256]{4,3,2,1,0:T(8,128)(2,1)} %param.5, pred[]{:T(512)} %bitcast.2), kind=kLoop, calls=%fused_computation.2 | loop fusion | flops 524288 | bytes 2097154 | tf_op jit(solution)/shard_map/jit(_where)/select_n | solution.py:248
  3.8 0.0 copy-start
  3.8 0.0 copy-start.1
  3.8 0.0 copy-start.2
  3.8 0.1 maximum_bitcast_fusion
  3.9 0.2 copy.5
  4.2 1.2 %copy-done = bf16[1,2,128,4096]{3,2,1,0:T(8,128)(2,1)S(1)} copy-done((bf16[1,2,128,4096]{3,2,1,0:T(8,128)(2,1)S(1)}, bf16[1,2,128,4096]{3,2,1,0:T(8,128)(2,1)}, u32[]{:S(2)}) %copy-start) | copy-done | bytes 2097176
  5.4 0.0 copy-done.1
  5.4 0.0 copy-done.2
  5.4 60.0 %relay_attention.1 = bf16[1,2,128,4096]{3,2,1,0:T(8,128)(2,1)S(1)} custom-call(s32[1,2,4]{2,1,0:T(2,128)S(1)} %copy-done.2, s32[1,2]{1,0:T(1,128)S(1)} %copy-done.1, bf16[1,2,128,4096]{3,2,1,0:T(8,128)(2,1)S(1)} %copy-done, bf16[16,128,256]{2,1,0:T(8,128)(2,1)S(1)} %bitcast.9), custom_call_target="tpu_custom_call" | custom-call | tf_op jit(solution)/shard_map/relay_attention/pallas_call | solution.py:253
  65.4 1.3 %copy.7 = bf16[1,2,128,4096]{3,2,1,0:T(8,128)(2,1)} copy(bf16[1,2,128,4096]{3,2,1,0:T(8,128)(2,1)S(1)} %relay_attention.1) | data formatting | bytes 4194304
Async XLA Ops:
  3.8 1.6 %copy-start = (bf16[1,2,128,4096]{3,2,1,0:T(8,128)(2,1)S(1)}, bf16[1,2,128,4096]{3,2,1,0:T(8,128)(2,1)}, u32[]{:S(2)}) copy-start(bf16[1,2,128,4096]{3,2,1,0:T(8,128)(2,1)} %q_hbm.1) | copy-start | bytes 6291460
  3.8 1.6 %copy-start.1 = (s32[1,2]{1,0:T(1,128)S(1)}, s32[1,2]{1,0:T(1,128)}, u32[]{:S(2)}) copy-start(s32[1,2]{1,0:T(1,128)} %order_ref.1) | copy-start | bytes 28
  3.8 1.6 %copy-start.2 = (s32[1,2,4]{2,1,0:T(2,128)S(1)}, s32[1,2,4]{2,1,0:T(2,128)}, u32[]{:S(2)}) copy-start(s32[1,2,4]{2,1,0:T(2,128)} %lengths_ref.1) | copy-start | bytes 100

commit v2 on v1

--- a/solution.py
+++ b/solution.py
@@ -22,6 +22,8 @@
     q_hbm,
     kv_hbm,
     out_hbm,
+    raw,
+    spread,
     kvbuf,
     qbuf,
     obuf,
@@ -45,6 +47,8 @@
     groups = chunks // micro
     out_cols = q_cols // groups
     share = out_cols // head
+    parts, part_cols = obuf.shape[1], obuf.shape[3]
+    part_heads = part_cols // head
     docs = lengths_ref.shape[2]
 
     me = lax.axis_index("seq")
@@ -61,12 +65,9 @@
     def slot(c, d):
         return kvbuf.at[c, pl.ds(d * tok, tok), :]
 
-    def source(c, k):
-        return kv_hbm.at[c] if k == 0 else slot(c, k * width)
-
     def column_copy(c, k):
         return pltpu.make_async_remote_copy(
-            src_ref=source(c, k),
+            src_ref=slot(c, k * width),
             dst_ref=slot(c, (k + 1) * width),
             send_sem=column_sem.at[k, c],
             recv_sem=recv_sem.at[(k + 1) * width, c],
@@ -77,7 +78,7 @@
     def row_copy(c, index):
         k, dx = row_moves[index]
         return pltpu.make_async_remote_copy(
-            src_ref=source(c, k),
+            src_ref=slot(c, k * width),
             dst_ref=slot(c, k * width + dx),
             send_sem=row_sem.at[index, c],
             recv_sem=recv_sem.at[k * width + dx, c],
@@ -85,13 +86,13 @@
             device_id_type=MESH,
         )
 
-    def out_copy(c):
-        columns = pl.ds(pl.multiple_of((c % groups) * out_cols, out_cols), out_cols)
+    def out_copy(c, part):
+        first = pl.multiple_of((c % groups) * out_cols + part * part_cols, part_cols)
         return pltpu.make_async_remote_copy(
-            src_ref=obuf.at[c],
-            dst_ref=out_hbm.at[0, c // groups, :, columns],
-            send_sem=osend_sem.at[c],
-            recv_sem=orecv_sem.at[c],
+            src_ref=obuf.at[c, part],
+            dst_ref=out_hbm.at[0, c // groups, :, pl.ds(first, part_cols)],
+            send_sem=osend_sem.at[part, c],
+            recv_sem=orecv_sem.at[part, c],
             device_id=((section + 1) % sections, me),
             device_id_type=MESH,
         )
@@ -133,10 +134,34 @@
     for step in (1, sections - 1):
         greet(me >= 0, ((section + step) % sections, me))
 
+    kv_copies = [
+        pltpu.make_async_copy(kv_hbm.at[0, m], raw.at[m], local_sem.at[1 + m]) for m in range(micro)
+    ]
     q_copy = pltpu.make_async_copy(q_hbm.at[0], qbuf, local_sem.at[0])
-    kv_copy = pltpu.make_async_copy(kv_hbm, kvbuf.at[:, pl.ds(0, tok), :], local_sem.at[1])
+    for copy in kv_copies:
+        copy.start()
     q_copy.start()
-    kv_copy.start()
+    for copy in kv_copies:
+        copy.wait()
+
+    def by_head(j):
+        for half in range(2):
+            columns = pl.ds(half * head, head)
+            one = raw[order_ref[0, j], :, :, columns]
+            spread[half] = one.astype(jnp.float32).reshape(tok * groups, head)
+            for g in range(groups):
+                kvbuf[j * groups + g, pl.ds(0, tok), columns] = spread[
+                    half, pl.ds(g, tok, stride=groups), :
+                ].astype(kvbuf.dtype)
+
+    lead = min(LEAD, groups)
+    by_head(0)
+    column_mates = jnp.where(z > 0, 1, 0) + jnp.where(z + 1 < depth, 1, 0)
+    pl.semaphore_wait(barrier, column_mates + (width - 1) + 2)
+    for c in range(lead):
+        start_sends(c, 0)
+    for j in range(1, micro):
+        by_head(j)
 
     for d in range(1, reach + 1):
 
@@ -161,34 +186,32 @@
             allowed = (other >= begin) & (other <= own)
             bias[j, :, pl.ds(d * tok, tok)] = jnp.where(allowed, 0.0, MASKED)
 
-    column_mates = jnp.where(z > 0, 1, 0) + jnp.where(z + 1 < depth, 1, 0)
-    pl.semaphore_wait(barrier, column_mates + (width - 1) + 2)
-
-    lead = min(LEAD, chunks)
-    for c in range(lead):
-        start_sends(c, 0)
     q_copy.wait()
-    kv_copy.wait()
-
     factor = head**-0.5 * math.log2(math.e)
 
     def compute(c):
         j = c // groups
-        columns = pl.ds(pl.multiple_of((c % groups) * out_cols, out_cols), out_cols)
-        q = qbuf[order_ref[0, j], :, columns]
-        rows = jnp.concatenate([q[:, h * head : (h + 1) * head] for h in range(share)], axis=0)
         k = kvbuf[c, :, :head]
         v = kvbuf[c, :, head:]
-        scores = lax.dot_general(
-            rows, k, (((1,), (1,)), ((), ())), preferred_element_type=jnp.float32
-        )
         hidden = bias[j]
-        for h in range(share):
-            part = scores[h * tok : (h + 1) * tok] * factor + hidden
-            weights = jnp.exp2(part - jnp.max(part, axis=1, keepdims=True))
-            totals = jnp.sum(weights, axis=1, keepdims=True)
-            mixed = jnp.dot(weights.astype(jnp.bfloat16), v, preferred_element_type=jnp.float32)
-            obuf[c, :, h * head : (h + 1) * head] = (mixed / totals).astype(obuf.dtype)
+        for part in range(parts):
+            first = pl.multiple_of((c % groups) * out_cols + part * part_cols, part_cols)
+            q = qbuf[order_ref[0, j], :, pl.ds(first, part_cols)]
+            rows = jnp.concatenate(
+                [q[:, h * head : (h + 1) * head] for h in range(part_heads)], axis=0
+            )
+            scores = lax.dot_general(
+                rows, k, (((1,), (1,)), ((), ())), preferred_element_type=jnp.float32
+            )
+            for h in range(part_heads):
+                logits = scores[h * tok : (h + 1) * tok] * factor + hidden
+                weights = jnp.exp2(logits - jnp.max(logits, axis=1, keepdims=True))
+                totals = jnp.sum(weights, axis=1, keepdims=True)
+                mixed = jnp.dot(
+                    weights.astype(jnp.bfloat16), v, preferred_element_type=jnp.float32
+                )
+                obuf[c, part, :, h * head : (h + 1) * head] = (mixed / totals).astype(obuf.dtype)
+            out_copy(c, part).start()
 
     def turn(t, carry):
         @pl.when(t + lead < chunks)
@@ -210,7 +233,6 @@
                 if d % width != 0:
                     arrived(c, d)
             compute(c)
-            out_copy(c).start()
 
         return carry
 
@@ -219,7 +241,8 @@
     def drain(c, carry):
         for k in range(hops + 1):
             each_send(c, k, lambda copy: copy.wait_send())
-        out_copy(c).wait()
+        for part in range(parts):
+            out_copy(c, part).wait()
         return carry
 
     lax.fori_loop(0, chunks, drain, 0)
@@ -241,14 +264,7 @@
         if dx != 0 and 1 <= k * width + dx <= reach
     )
 
-    picked = []
-    for j in range(micro):
-        one = keys_values[0, 0]
-        for m in range(1, micro):
-            one = jnp.where(order[0, j] == m, keys_values[0, m], one)
-        picked.append(one)
-    pairs = jnp.stack(picked).transpose(0, 2, 1, 3).reshape(chunks, tok, pair)
-
+    parts = 2 if (out_cols // (pair // 2)) % 2 == 0 else 1
     keys = (reach + 1) * tok
     return pl.pallas_call(
         kernel,
@@ -256,29 +272,31 @@
         in_specs=[
             pl.BlockSpec(memory_space=pltpu.SMEM),
             pl.BlockSpec(memory_space=pltpu.SMEM),
-            pl.BlockSpec(memory_space=pl.ANY),
-            pl.BlockSpec(memory_space=pl.ANY),
+            pl.BlockSpec(memory_space=pltpu.HBM),
+            pl.BlockSpec(memory_space=pltpu.HBM),
         ],
         out_specs=pl.BlockSpec(memory_space=pl.ANY),
         scratch_shapes=[
+            pltpu.VMEM((micro, tok, groups, pair), jnp.bfloat16),
+            pltpu.VMEM((2, tok * groups, pair // 2), jnp.float32),
             pltpu.VMEM((chunks, keys, pair), jnp.bfloat16),
             pltpu.VMEM((micro, tok, q_cols), jnp.bfloat16),
-            pltpu.VMEM((chunks, tok, out_cols), jnp.bfloat16),
+            pltpu.VMEM((chunks, parts, tok, out_cols // parts), jnp.bfloat16),
             pltpu.VMEM((micro, tok, keys), jnp.float32),
-            pltpu.SemaphoreType.DMA((2,)),
+            pltpu.SemaphoreType.DMA((1 + micro,)),
             pltpu.SemaphoreType.DMA((reach + 1, chunks)),
             pltpu.SemaphoreType.DMA((hops, chunks)),
             pltpu.SemaphoreType.DMA((max(1, moves), chunks)),
-            pltpu.SemaphoreType.DMA((chunks,)),
-            pltpu.SemaphoreType.DMA((chunks,)),
+            pltpu.SemaphoreType.DMA((parts, chunks)),
+            pltpu.SemaphoreType.DMA((parts, chunks)),
         ],
         compiler_params=pltpu.CompilerParams(
             collective_id=0,
             has_side_effects=True,
-            vmem_limit_bytes=48 * 1024 * 1024,
+            vmem_limit_bytes=60 * 1024 * 1024,
         ),
         name="relay_attention",
-    )(lengths, order, queries, pairs)
+    )(lengths, order, queries, keys_values)
 
 
 def solution(mesh):

time: 66.9 us -> 64.1 us (0.958)
  other arithmetic: 1.37 us -> 0 us
  between operations: 1.27 us -> 0.01 us
  local copies, waits for them, and re-layouts: 4.09 us -> 3.13 us
    slice x1 -> x0, local copies, waits for them, and re-layouts: 1.3 us -> none  [local(): one = jnp.where(order[0, j] == m, keys_values[0, m], one)]
    select_n x1 -> x0, other arithmetic: 1.27 us -> none  [local(): one = jnp.where(order[0, j] == m, keys_values[0, m], one)]
    unnamed x7 -> x1, local copies, waits for them, and re-layouts: 2.56 us -> 3.13 us
where the time goes in v2:
time: 64.1 us; the launch traced here: 63.7 us
  Pallas kernels  60.5 us (94%)
  local copies, waits for them, and re-layouts  3.13 us (5%)
    pallas_call x1, Pallas kernels, local(): pl.pallas_call(kernel, out_shape=jax.ShapeDtypeStruct(queries.shape, quer...  60.5 us
    unnamed x1, local copies, waits for them, and re-layouts  3.13 us

profile of v2, /device:TPU:24, one launch (start us, length us, event | category | flops | bytes accessed | tf_op | source)
XLA Modules:
  0.0 63.7 jit_solution(4308840026736753334)
XLA Ops:
  0.0 60.5 %relay_attention.1 = bf16[1,2,128,4096]{3,2,1,0:T(8,128)(2,1)} custom-call(s32[1,2,4]{2,1,0:T(2,128)} %lengths_ref.1, s32[1,2]{1,0:T(1,128)} %order_ref.1, bf16[1,2,128,4096]{3,2,1,0:T(8,128)(2,1)} %q_hbm.1, bf16[1,2,128,8,256]{4,3,2,1,0:T(8,128)(2,1)} %kv_hbm.1), custom_call_target="tpu_custom_call" | custom-call | tf_op jit(solution)/shard_map/relay_attention/pallas_call | solution.py:269
  60.5 3.1 %copy.6 = bf16[1,2,128,4096]{3,2,1,0:T(8,128)(2,1)} copy(bf16[1,2,128,4096]{3,2,1,0:T(8,128)(2,1)} %relay_attention.1) | data formatting | bytes 4194304

commit v3 on v2

--- a/solution.py
+++ b/solution.py
@@ -42,13 +42,14 @@
     reach = n // 2
     hops = -(-reach // width)
     micro, tok, q_cols = qbuf.shape
+    pieces = recv_sem.shape[1]
+    rows = tok // pieces
     chunks, keys, pair = kvbuf.shape
     head = pair // 2
     groups = chunks // micro
     out_cols = q_cols // groups
     share = out_cols // head
-    parts, part_cols = obuf.shape[1], obuf.shape[3]
-    part_heads = part_cols // head
+    joint = 2 if share % 2 == 0 else 1
     docs = lengths_ref.shape[2]
 
     me = lax.axis_index("seq")
@@ -62,62 +63,62 @@
         if dx != 0 and 1 <= k * width + dx <= reach
     ]
 
-    def slot(c, d):
-        return kvbuf.at[c, pl.ds(d * tok, tok), :]
-
-    def column_copy(c, k):
+    def slot(c, d, p):
+        return kvbuf.at[c, pl.ds(d * tok + p * rows, rows), :]
+
+    def column_copy(c, k, p):
         return pltpu.make_async_remote_copy(
-            src_ref=slot(c, k * width),
-            dst_ref=slot(c, (k + 1) * width),
-            send_sem=column_sem.at[k, c],
-            recv_sem=recv_sem.at[(k + 1) * width, c],
+            src_ref=slot(c, k * width, p),
+            dst_ref=slot(c, (k + 1) * width, p),
+            send_sem=column_sem.at[k, p, c],
+            recv_sem=recv_sem.at[(k + 1) * width, p, c],
             device_id=(section, me + width),
             device_id_type=MESH,
         )
 
-    def row_copy(c, index):
+    def row_copy(c, index, p):
         k, dx = row_moves[index]
         return pltpu.make_async_remote_copy(
-            src_ref=slot(c, k * width),
-            dst_ref=slot(c, k * width + dx),
-            send_sem=row_sem.at[index, c],
-            recv_sem=recv_sem.at[k * width + dx, c],
+            src_ref=slot(c, k * width, p),
+            dst_ref=slot(c, k * width + dx, p),
+            send_sem=row_sem.at[index, p, c],
+            recv_sem=recv_sem.at[k * width + dx, p, c],
             device_id=(section, me + dx),
             device_id_type=MESH,
         )
 
-    def out_copy(c, part):
-        first = pl.multiple_of((c % groups) * out_cols + part * part_cols, part_cols)
+    def out_copy(c, h):
+        first = pl.multiple_of((c % groups) * out_cols + h * head, head)
         return pltpu.make_async_remote_copy(
-            src_ref=obuf.at[c, part],
-            dst_ref=out_hbm.at[0, c // groups, :, pl.ds(first, part_cols)],
-            send_sem=osend_sem.at[part, c],
-            recv_sem=orecv_sem.at[part, c],
+            src_ref=obuf.at[c, h],
+            dst_ref=out_hbm.at[0, c // groups, :, pl.ds(first, head)],
+            send_sem=osend_sem.at[h, c],
+            recv_sem=orecv_sem.at[h, c],
             device_id=((section + 1) % sections, me),
             device_id_type=MESH,
         )
 
-    def each_send(c, k, act):
+    def each_send(c, k, p, act):
         if k < hops and (k + 1) * width <= reach:
 
             @pl.when((z + 1 < depth) & (z >= k))
             def _():
-                act(column_copy(c, k))
+                act(column_copy(c, k, p))
 
         for index, (move_k, dx) in enumerate(row_moves):
             if move_k == k:
 
                 @pl.when((x + dx >= 0) & (x + dx < width) & (z >= k))
                 def _(index=index):
-                    act(row_copy(c, index))
-
-    def start_sends(c, k):
-        each_send(c, k, lambda copy: copy.start())
-
-    def arrived(c, d):
+                    act(row_copy(c, index, p))
+
+    def start_sends(c, k, p):
+        each_send(c, k, p, lambda copy: copy.start())
+
+    def arrived(c, d, p):
         @pl.when(me >= d)
         def _():
-            pltpu.make_async_copy(slot(c, d), slot(c, d), recv_sem.at[d, c]).wait()
+            pltpu.make_async_copy(slot(c, d, p), slot(c, d, p), recv_sem.at[d, p, c]).wait()
 
     barrier = pltpu.get_barrier_semaphore()
 
@@ -159,7 +160,8 @@
     column_mates = jnp.where(z > 0, 1, 0) + jnp.where(z + 1 < depth, 1, 0)
     pl.semaphore_wait(barrier, column_mates + (width - 1) + 2)
     for c in range(lead):
-        start_sends(c, 0)
+        for p in range(pieces):
+            start_sends(c, 0, p)
     for j in range(1, micro):
         by_head(j)
 
@@ -194,44 +196,47 @@
         k = kvbuf[c, :, :head]
         v = kvbuf[c, :, head:]
         hidden = bias[j]
-        for part in range(parts):
-            first = pl.multiple_of((c % groups) * out_cols + part * part_cols, part_cols)
-            q = qbuf[order_ref[0, j], :, pl.ds(first, part_cols)]
-            rows = jnp.concatenate(
-                [q[:, h * head : (h + 1) * head] for h in range(part_heads)], axis=0
+        for pair_first in range(0, share, joint):
+            first = pl.multiple_of((c % groups) * out_cols + pair_first * head, joint * head)
+            q = qbuf[order_ref[0, j], :, pl.ds(first, joint * head)]
+            stacked = jnp.concatenate(
+                [q[:, i * head : (i + 1) * head] for i in range(joint)], axis=0
             )
             scores = lax.dot_general(
-                rows, k, (((1,), (1,)), ((), ())), preferred_element_type=jnp.float32
+                stacked, k, (((1,), (1,)), ((), ())), preferred_element_type=jnp.float32
             )
-            for h in range(part_heads):
-                logits = scores[h * tok : (h + 1) * tok] * factor + hidden
+            for i in range(joint):
+                logits = scores[i * tok : (i + 1) * tok] * factor + hidden
                 weights = jnp.exp2(logits - jnp.max(logits, axis=1, keepdims=True))
                 totals = jnp.sum(weights, axis=1, keepdims=True)
                 mixed = jnp.dot(
                     weights.astype(jnp.bfloat16), v, preferred_element_type=jnp.float32
                 )
-                obuf[c, part, :, h * head : (h + 1) * head] = (mixed / totals).astype(obuf.dtype)
-            out_copy(c, part).start()
+                obuf[c, pair_first + i] = (mixed / totals).astype(obuf.dtype)
+                out_copy(c, pair_first + i).start()
 
     def turn(t, carry):
         @pl.when(t + lead < chunks)
         def _():
-            start_sends(t + lead, 0)
+            for p in range(pieces):
+                start_sends(t + lead, 0, p)
 
         for k in range(1, hops + 1):
             if k * width <= reach:
 
                 @pl.when((t - (k - 1) >= 0) & (t - (k - 1) < chunks))
                 def _(k=k):
-                    arrived(t - (k - 1), k * width)
-                    start_sends(t - (k - 1), k)
+                    for p in range(pieces):
+                        arrived(t - (k - 1), k * width, p)
+                        start_sends(t - (k - 1), k, p)
 
         @pl.when(t >= hops)
         def _():
             c = t - hops
             for d in range(1, reach + 1):
                 if d % width != 0:
-                    arrived(c, d)
+                    for p in range(pieces):
+                        arrived(c, d, p)
             compute(c)
 
         return carry
@@ -240,9 +245,10 @@
 
     def drain(c, carry):
         for k in range(hops + 1):
-            each_send(c, k, lambda copy: copy.wait_send())
-        for part in range(parts):
-            out_copy(c, part).wait()
+            for p in range(pieces):
+                each_send(c, k, p, lambda copy: copy.wait_send())
+        for h in range(share):
+            out_copy(c, h).wait()
         return carry
 
     lax.fori_loop(0, chunks, drain, 0)
@@ -264,8 +270,11 @@
         if dx != 0 and 1 <= k * width + dx <= reach
     )
 
-    parts = 2 if (out_cols // (pair // 2)) % 2 == 0 else 1
+    head = pair // 2
+    share = out_cols // head
+    pieces = 2 if tok % 32 == 0 else 1
     keys = (reach + 1) * tok
+    inputs = [pltpu.with_memory_space_constraint(a, pltpu.HBM) for a in (queries, keys_values)]
     return pl.pallas_call(
         kernel,
         out_shape=jax.ShapeDtypeStruct(queries.shape, queries.dtype),
@@ -281,22 +290,22 @@
             pltpu.VMEM((2, tok * groups, pair // 2), jnp.float32),
             pltpu.VMEM((chunks, keys, pair), jnp.bfloat16),
             pltpu.VMEM((micro, tok, q_cols), jnp.bfloat16),
-            pltpu.VMEM((chunks, parts, tok, out_cols // parts), jnp.bfloat16),
+            pltpu.VMEM((chunks, share, tok, head), jnp.bfloat16),
             pltpu.VMEM((micro, tok, keys), jnp.float32),
             pltpu.SemaphoreType.DMA((1 + micro,)),
-            pltpu.SemaphoreType.DMA((reach + 1, chunks)),
-            pltpu.SemaphoreType.DMA((hops, chunks)),
-            pltpu.SemaphoreType.DMA((max(1, moves), chunks)),
-            pltpu.SemaphoreType.DMA((parts, chunks)),
-            pltpu.SemaphoreType.DMA((parts, chunks)),
+            pltpu.SemaphoreType.DMA((reach + 1, pieces, chunks)),
+            pltpu.SemaphoreType.DMA((hops, pieces, chunks)),
+            pltpu.SemaphoreType.DMA((max(1, moves), pieces, chunks)),
+            pltpu.SemaphoreType.DMA((share, chunks)),
+            pltpu.SemaphoreType.DMA((share, chunks)),
         ],
         compiler_params=pltpu.CompilerParams(
             collective_id=0,
             has_side_effects=True,
-            vmem_limit_bytes=60 * 1024 * 1024,
+            vmem_limit_bytes=40 * 1024 * 1024,
         ),
         name="relay_attention",
-    )(lengths, order, queries, keys_values)
+    )(lengths, order, *inputs)
 
 
 def solution(mesh):

time: 64.1 us -> 65.2 us (1.017)
  Pallas kernels: 60.5 us -> 61.9 us
    pallas_call x1, Pallas kernels: 60.5 us -> 61.9 us  [local(): pl.pallas_call(kernel, out_shape=jax.ShapeDtypeStruct(queries.shape, quer...]
    unnamed x1 -> x5, local copies, waits for them, and re-layouts: 3.13 us -> 2.65 us
where the time goes in v3:
time: 65.2 us; the launch traced here: 64.6 us
  Pallas kernels  61.9 us (95%)
  local copies, waits for them, and re-layouts  2.65 us (4%)
    pallas_call x1, Pallas kernels, local(): pl.pallas_call(kernel, out_shape=jax.ShapeDtypeStruct(queries.shape, quer...  61.9 us
    unnamed x5, local copies, waits for them, and re-layouts  2.65 us

profile of v3, /device:TPU:24, one launch (start us, length us, event | category | flops | bytes accessed | tf_op | source)
XLA Modules:
  0.0 64.6 jit_solution(17357640924303465945)
XLA Ops:
  0.0 0.0 copy-start
  0.0 0.7 %copy-done = s32[1,2,4]{2,1,0:T(2,128)S(1)} copy-done((s32[1,2,4]{2,1,0:T(2,128)S(1)}, s32[1,2,4]{2,1,0:T(2,128)}, u32[]{:S(2)}) %copy-start) | copy-done | bytes 56
  0.7 0.0 copy-start.1
  0.7 0.7 %copy-done.1 = s32[1,2]{1,0:T(1,128)S(1)} copy-done((s32[1,2]{1,0:T(1,128)S(1)}, s32[1,2]{1,0:T(1,128)}, u32[]{:S(2)}) %copy-start.1) | copy-done | bytes 32
  1.3 61.9 %relay_attention.1 = bf16[1,2,128,4096]{3,2,1,0:T(8,128)(2,1)S(1)} custom-call(s32[1,2,4]{2,1,0:T(2,128)S(1)} %copy-done, s32[1,2]{1,0:T(1,128)S(1)} %copy-done.1, bf16[1,2,128,4096]{3,2,1,0:T(8,128)(2,1)} %q_hbm.1, bf16[1,2,128,8,256]{4,3,2,1,0:T(8,128)(2,1)} %kv_hbm.1), custom_call_target="tpu_custom_call" | custom-call | tf_op jit(solution)/shard_map/relay_attention/pallas_call | solution.py:278
  63.3 1.3 %copy.6 = bf16[1,2,128,4096]{3,2,1,0:T(8,128)(2,1)} copy(bf16[1,2,128,4096]{3,2,1,0:T(8,128)(2,1)S(1)} %relay_attention.1) | data formatting | bytes 4194304
Async XLA Ops:
  0.0 0.7 %copy-start = (s32[1,2,4]{2,1,0:T(2,128)S(1)}, s32[1,2,4]{2,1,0:T(2,128)}, u32[]{:S(2)}) copy-start(s32[1,2,4]{2,1,0:T(2,128)} %lengths_ref.1) | copy-start | bytes 100
  0.7 0.7 %copy-start.1 = (s32[1,2]{1,0:T(1,128)S(1)}, s32[1,2]{1,0:T(1,128)}, u32[]{:S(2)}) copy-start(s32[1,2]{1,0:T(1,128)} %order_ref.1) | copy-start | bytes 28

commit v4 on v3

--- a/solution.py
+++ b/solution.py
@@ -49,7 +49,9 @@
     groups = chunks // micro
     out_cols = q_cols // groups
     share = out_cols // head
-    joint = 2 if share % 2 == 0 else 1
+    parts, part_cols = obuf.shape[1], obuf.shape[3]
+    joint = part_cols // head
+    block = tok // 2
     docs = lengths_ref.shape[2]
 
     me = lax.axis_index("seq")
@@ -87,13 +89,13 @@
             device_id_type=MESH,
         )
 
-    def out_copy(c, h):
-        first = pl.multiple_of((c % groups) * out_cols + h * head, head)
+    def out_copy(c, part):
+        first = pl.multiple_of((c % groups) * out_cols + part * part_cols, part_cols)
         return pltpu.make_async_remote_copy(
-            src_ref=obuf.at[c, h],
-            dst_ref=out_hbm.at[0, c // groups, :, pl.ds(first, head)],
-            send_sem=osend_sem.at[h, c],
-            recv_sem=orecv_sem.at[h, c],
+            src_ref=obuf.at[c, part],
+            dst_ref=out_hbm.at[0, c // groups, :, pl.ds(first, part_cols)],
+            send_sem=osend_sem.at[part, c],
+            recv_sem=orecv_sem.at[part, c],
             device_id=((section + 1) % sections, me),
             device_id_type=MESH,
         )
@@ -194,26 +196,29 @@
     def compute(c):
         j = c // groups
         k = kvbuf[c, :, :head]
-        v = kvbuf[c, :, head:]
-        hidden = bias[j]
-        for pair_first in range(0, share, joint):
-            first = pl.multiple_of((c % groups) * out_cols + pair_first * head, joint * head)
-            q = qbuf[order_ref[0, j], :, pl.ds(first, joint * head)]
+        v = jnp.concatenate([kvbuf[c, :, head:], jnp.ones((keys, head), kvbuf.dtype)], axis=1)
+        for part in range(parts):
+            first = pl.multiple_of((c % groups) * out_cols + part * part_cols, part_cols)
+            q = qbuf[order_ref[0, j], :, pl.ds(first, part_cols)]
             stacked = jnp.concatenate(
                 [q[:, i * head : (i + 1) * head] for i in range(joint)], axis=0
             )
             scores = lax.dot_general(
                 stacked, k, (((1,), (1,)), ((), ())), preferred_element_type=jnp.float32
             )
+            weights = []
+            for top in range(0, joint * tok, block):
+                hidden = bias[j, pl.ds(top % tok, block), :]
+                logits = scores[top : top + block] * factor + hidden
+                lifted = logits - jnp.max(logits, axis=1, keepdims=True)
+                weights.append(jnp.exp2(lifted).astype(jnp.bfloat16))
+            mixed = jnp.dot(
+                jnp.concatenate(weights, axis=0), v, preferred_element_type=jnp.float32
+            )
+            result = (mixed[:, :head] / mixed[:, head:]).astype(obuf.dtype)
             for i in range(joint):
-                logits = scores[i * tok : (i + 1) * tok] * factor + hidden
-                weights = jnp.exp2(logits - jnp.max(logits, axis=1, keepdims=True))
-                totals = jnp.sum(weights, axis=1, keepdims=True)
-                mixed = jnp.dot(
-                    weights.astype(jnp.bfloat16), v, preferred_element_type=jnp.float32
-                )
-                obuf[c, pair_first + i] = (mixed / totals).astype(obuf.dtype)
-                out_copy(c, pair_first + i).start()
+                obuf[c, part, :, i * head : (i + 1) * head] = result[i * tok : (i + 1) * tok]
+            out_copy(c, part).start()
 
     def turn(t, carry):
         @pl.when(t + lead < chunks)
@@ -247,8 +252,8 @@
         for k in range(hops + 1):
             for p in range(pieces):
                 each_send(c, k, p, lambda copy: copy.wait_send())
-        for h in range(share):
-            out_copy(c, h).wait()
+        for part in range(parts):
+            out_copy(c, part).wait()
         return carry
 
     lax.fori_loop(0, chunks, drain, 0)
@@ -272,9 +277,13 @@
 
     head = pair // 2
     share = out_cols // head
-    pieces = 2 if tok % 32 == 0 else 1
+    joint = 2 if share % 2 == 0 else 1
+    pieces = 1
     keys = (reach + 1) * tok
-    inputs = [pltpu.with_memory_space_constraint(a, pltpu.HBM) for a in (queries, keys_values)]
+    inputs = [
+        pltpu.with_memory_space_constraint(a, pltpu.HBM)
+        for a in (lengths, order, queries, keys_values)
+    ]
     return pl.pallas_call(
         kernel,
         out_shape=jax.ShapeDtypeStruct(queries.shape, queries.dtype),
@@ -290,14 +299,14 @@
             pltpu.VMEM((2, tok * groups, pair // 2), jnp.float32),
             pltpu.VMEM((chunks, keys, pair), jnp.bfloat16),
             pltpu.VMEM((micro, tok, q_cols), jnp.bfloat16),
-            pltpu.VMEM((chunks, share, tok, head), jnp.bfloat16),
+            pltpu.VMEM((chunks, share // joint, tok, joint * head), jnp.bfloat16),
             pltpu.VMEM((micro, tok, keys), jnp.float32),
             pltpu.SemaphoreType.DMA((1 + micro,)),
             pltpu.SemaphoreType.DMA((reach + 1, pieces, chunks)),
             pltpu.SemaphoreType.DMA((hops, pieces, chunks)),
             pltpu.SemaphoreType.DMA((max(1, moves), pieces, chunks)),
-            pltpu.SemaphoreType.DMA((share, chunks)),
-            pltpu.SemaphoreType.DMA((share, chunks)),
+            pltpu.SemaphoreType.DMA((share // joint, chunks)),
+            pltpu.SemaphoreType.DMA((share // joint, chunks)),
         ],
         compiler_params=pltpu.CompilerParams(
             collective_id=0,
@@ -305,7 +314,7 @@
             vmem_limit_bytes=40 * 1024 * 1024,
         ),
         name="relay_attention",
-    )(lengths, order, *inputs)
+    )(*inputs)
 
 
 def solution(mesh):

time: 65.2 us -> 62.9 us (0.965)
  local copies, waits for them, and re-layouts: 2.65 us -> 1.32 us
  Pallas kernels: 61.9 us -> 60.8 us
    unnamed x5 -> x1, local copies, waits for them, and re-layouts: 2.65 us -> 1.32 us
    pallas_call x1, Pallas kernels: 61.9 us -> 60.8 us  [local(): pl.pallas_call(kernel, out_shape=jax.ShapeDtypeStruct(queries.shape, quer...]
where the time goes in v4:
time: 62.9 us; the launch traced here: 62.2 us
  Pallas kernels  60.8 us (97%)
  local copies, waits for them, and re-layouts  1.32 us (2%)
    pallas_call x1, Pallas kernels, local(): pl.pallas_call(kernel, out_shape=jax.ShapeDtypeStruct(queries.shape, quer...  60.8 us
    unnamed x1, local copies, waits for them, and re-layouts  1.32 us

profile of v4, /device:TPU:24, one launch (start us, length us, event | category | flops | bytes accessed | tf_op | source)
XLA Modules:
  0.0 62.2 jit_solution(12241093131152173737)
XLA Ops:
  0.0 60.8 %relay_attention.1 = bf16[1,2,128,4096]{3,2,1,0:T(8,128)(2,1)S(1)} custom-call(s32[1,2,4]{2,1,0:T(2,128)} %lengths_ref.1, s32[1,2]{1,0:T(1,128)} %order_ref.1, bf16[1,2,128,4096]{3,2,1,0:T(8,128)(2,1)} %q_hbm.1, bf16[1,2,128,8,256]{4,3,2,1,0:T(8,128)(2,1)} %kv_hbm.1), custom_call_target="tpu_custom_call" | custom-call | tf_op jit(solution)/shard_map/relay_attention/pallas_call | solution.py:287
  60.9 1.3 %copy.6 = bf16[1,2,128,4096]{3,2,1,0:T(8,128)(2,1)} copy(bf16[1,2,128,4096]{3,2,1,0:T(8,128)(2,1)S(1)} %relay_attention.1) | data formatting | bytes 4194304

commit v5 on v4

--- a/solution.py
+++ b/solution.py
@@ -42,8 +42,6 @@
     reach = n // 2
     hops = -(-reach // width)
     micro, tok, q_cols = qbuf.shape
-    pieces = recv_sem.shape[1]
-    rows = tok // pieces
     chunks, keys, pair = kvbuf.shape
     head = pair // 2
     groups = chunks // micro
@@ -53,6 +51,8 @@
     joint = part_cols // head
     block = tok // 2
     docs = lengths_ref.shape[2]
+    last = chunks - 1
+    halves = 2 if tok % 32 == 0 else 1
 
     me = lax.axis_index("seq")
     section = lax.axis_index("section")
@@ -66,14 +66,18 @@
     ]
 
     def slot(c, d, p):
-        return kvbuf.at[c, pl.ds(d * tok + p * rows, rows), :]
+        rows = tok if p is None else tok // halves
+        return kvbuf.at[c, pl.ds(d * tok + (p or 0) * rows, rows), :]
+
+    def arrival(c, d, p):
+        return recv_sem.at[d, chunks if p == 1 else c]
 
     def column_copy(c, k, p):
         return pltpu.make_async_remote_copy(
             src_ref=slot(c, k * width, p),
             dst_ref=slot(c, (k + 1) * width, p),
-            send_sem=column_sem.at[k, p, c],
-            recv_sem=recv_sem.at[(k + 1) * width, p, c],
+            send_sem=column_sem.at[k],
+            recv_sem=arrival(c, (k + 1) * width, p),
             device_id=(section, me + width),
             device_id_type=MESH,
         )
@@ -83,8 +87,8 @@
         return pltpu.make_async_remote_copy(
             src_ref=slot(c, k * width, p),
             dst_ref=slot(c, k * width + dx, p),
-            send_sem=row_sem.at[index, p, c],
-            recv_sem=recv_sem.at[k * width + dx, p, c],
+            send_sem=row_sem.at[index],
+            recv_sem=arrival(c, k * width + dx, p),
             device_id=(section, me + dx),
             device_id_type=MESH,
         )
@@ -94,33 +98,64 @@
         return pltpu.make_async_remote_copy(
             src_ref=obuf.at[c, part],
             dst_ref=out_hbm.at[0, c // groups, :, pl.ds(first, part_cols)],
-            send_sem=osend_sem.at[part, c],
-            recv_sem=orecv_sem.at[part, c],
+            send_sem=osend_sem,
+            recv_sem=orecv_sem,
             device_id=((section + 1) % sections, me),
             device_id_type=MESH,
         )
 
-    def each_send(c, k, p, act):
+    def by_piece(c, d, act):
+        if d <= (hops - 1) * width:
+            act(None)
+            return
+
+        @pl.when(c < last)
+        def _():
+            act(None)
+
+        @pl.when(c == last)
+        def _():
+            for p in range(halves):
+                act(p)
+
+    def column_goes(k):
+        return (z + 1 < depth) & (z >= k)
+
+    def row_goes(index):
+        k, dx = row_moves[index]
+        return (x + dx >= 0) & (x + dx < width) & (z >= k)
+
+    def each_send(k, act):
         if k < hops and (k + 1) * width <= reach:
 
-            @pl.when((z + 1 < depth) & (z >= k))
+            @pl.when(column_goes(k))
             def _():
-                act(column_copy(c, k, p))
+                act(column_copy, k, (k + 1) * width)
 
         for index, (move_k, dx) in enumerate(row_moves):
             if move_k == k:
 
-                @pl.when((x + dx >= 0) & (x + dx < width) & (z >= k))
-                def _(index=index):
-                    act(row_copy(c, index, p))
-
-    def start_sends(c, k, p):
-        each_send(c, k, p, lambda copy: copy.start())
+                @pl.when(row_goes(index))
+                def _(index=index, dx=dx):
+                    act(row_copy, index, k * width + dx)
+
+    def start_sends(c, k, p=None):
+        if p is None:
+            each_send(k, lambda copy, i, d: by_piece(c, d, lambda q: copy(c, i, q).start()))
+        else:
+            each_send(k, lambda copy, i, d: copy(c, i, p).start())
 
     def arrived(c, d, p):
         @pl.when(me >= d)
         def _():
-            pltpu.make_async_copy(slot(c, d, p), slot(c, d, p), recv_sem.at[d, p, c]).wait()
+            pltpu.make_async_copy(slot(c, d, p), slot(c, d, p), arrival(c, d, p)).wait()
+
+    def arrived_and_on(c, k):
+        def act(p):
+            arrived(c, k * width, p)
+            start_sends(c, k, p)
+
+        by_piece(c, k * width, act)
 
     barrier = pltpu.get_barrier_semaphore()
 
@@ -147,25 +182,30 @@
     for copy in kv_copies:
         copy.wait()
 
-    def by_head(j):
+    def by_head(j, then):
         for half in range(2):
-            columns = pl.ds(half * head, head)
-            one = raw[order_ref[0, j], :, :, columns]
+            one = raw[order_ref[0, j], :, :, pl.ds(half * head, head)]
             spread[half] = one.astype(jnp.float32).reshape(tok * groups, head)
-            for g in range(groups):
-                kvbuf[j * groups + g, pl.ds(0, tok), columns] = spread[
+        for g in range(groups):
+            for half in range(2):
+                kvbuf[j * groups + g, pl.ds(0, tok), pl.ds(half * head, head)] = spread[
                     half, pl.ds(g, tok, stride=groups), :
                 ].astype(kvbuf.dtype)
-
-    lead = min(LEAD, groups)
-    by_head(0)
-    column_mates = jnp.where(z > 0, 1, 0) + jnp.where(z + 1 < depth, 1, 0)
-    pl.semaphore_wait(barrier, column_mates + (width - 1) + 2)
-    for c in range(lead):
-        for p in range(pieces):
-            start_sends(c, 0, p)
+            then(g)
+
+    leads = [min(LEAD, groups), min(2, groups), 1]
+    turns = [0, chunks // 2, chunks * 3 // 4, chunks]
+
+    def first_sends(g):
+        if g == 0:
+            column_mates = jnp.where(z > 0, 1, 0) + jnp.where(z + 1 < depth, 1, 0)
+            pl.semaphore_wait(barrier, column_mates + (width - 1) + 2)
+        if g < leads[0]:
+            start_sends(jnp.int32(g), 0)
+
+    by_head(0, first_sends)
     for j in range(1, micro):
-        by_head(j)
+        by_head(j, lambda g: None)
 
     for d in range(1, reach + 1):
 
@@ -221,42 +261,53 @@
             out_copy(c, part).start()
 
     def turn(t, carry):
-        @pl.when(t + lead < chunks)
-        def _():
-            for p in range(pieces):
-                start_sends(t + lead, 0, p)
+        for lead, begin, end in zip(leads, turns, turns[1:]):
+            begin = max(begin, leads[0])
+
+            @pl.when((t + lead >= begin) & (t + lead < end))
+            def _(lead=lead):
+                start_sends(t + lead, 0)
 
         for k in range(1, hops + 1):
             if k * width <= reach:
 
                 @pl.when((t - (k - 1) >= 0) & (t - (k - 1) < chunks))
                 def _(k=k):
-                    for p in range(pieces):
-                        arrived(t - (k - 1), k * width, p)
-                        start_sends(t - (k - 1), k, p)
+                    arrived_and_on(t - (k - 1), k)
 
         @pl.when(t >= hops)
         def _():
             c = t - hops
             for d in range(1, reach + 1):
                 if d % width != 0:
-                    for p in range(pieces):
-                        arrived(c, d, p)
+                    by_piece(c, d, lambda p, d=d: arrived(c, d, p))
             compute(c)
 
         return carry
 
     lax.fori_loop(0, chunks + hops, turn, 0)
 
-    def drain(c, carry):
-        for k in range(hops + 1):
-            for p in range(pieces):
-                each_send(c, k, p, lambda copy: copy.wait_send())
-        for part in range(parts):
-            out_copy(c, part).wait()
-        return carry
-
-    lax.fori_loop(0, chunks, drain, 0)
+    def sent(ref, sem):
+        pltpu.make_async_copy(ref, ref, sem).wait()
+
+    def drained(k):
+        return kvbuf.at[:, pl.ds(k * width * tok, tok), :]
+
+    for k in range(hops):
+        if (k + 1) * width <= reach:
+
+            @pl.when(column_goes(k))
+            def _(k=k):
+                sent(drained(k), column_sem.at[k])
+
+    for index, (k, _) in enumerate(row_moves):
+
+        @pl.when(row_goes(index))
+        def _(k=k, index=index):
+            sent(drained(k), row_sem.at[index])
+
+    sent(obuf, osend_sem)
+    sent(out_hbm.at[0], orecv_sem)
 
 
 def local(queries, keys_values, lengths, order):
@@ -278,7 +329,6 @@
     head = pair // 2
     share = out_cols // head
     joint = 2 if share % 2 == 0 else 1
-    pieces = 1
     keys = (reach + 1) * tok
     inputs = [
         pltpu.with_memory_space_constraint(a, pltpu.HBM)
@@ -302,11 +352,11 @@
             pltpu.VMEM((chunks, share // joint, tok, joint * head), jnp.bfloat16),
             pltpu.VMEM((micro, tok, keys), jnp.float32),
             pltpu.SemaphoreType.DMA((1 + micro,)),
-            pltpu.SemaphoreType.DMA((reach + 1, pieces, chunks)),
-            pltpu.SemaphoreType.DMA((hops, pieces, chunks)),
-            pltpu.SemaphoreType.DMA((max(1, moves), pieces, chunks)),
-            pltpu.SemaphoreType.DMA((share // joint, chunks)),
-            pltpu.SemaphoreType.DMA((share // joint, chunks)),
+            pltpu.SemaphoreType.DMA((reach + 1, chunks + 1)),
+            pltpu.SemaphoreType.DMA((hops,)),
+            pltpu.SemaphoreType.DMA((max(1, moves),)),
+            pltpu.SemaphoreType.DMA(()),
+            pltpu.SemaphoreType.DMA(()),
         ],
         compiler_params=pltpu.CompilerParams(
             collective_id=0,

time: 62.9 us -> 61.6 us (0.979)
  Pallas kernels: 60.8 us -> 59.6 us
    pallas_call x1, Pallas kernels: 60.8 us -> 59.6 us  [local(): pl.pallas_call(kernel, out_shape=jax.ShapeDtypeStruct(queries.shape, quer...]
where the time goes in v5:
time: 61.6 us; the launch traced here: 60.9 us
  Pallas kernels  59.6 us (97%)
  local copies, waits for them, and re-layouts  1.32 us (2%)
    pallas_call x1, Pallas kernels, local(): pl.pallas_call(kernel, out_shape=jax.ShapeDtypeStruct(queries.shape, quer...  59.6 us
    unnamed x1, local copies, waits for them, and re-layouts  1.32 us

profile of v5, /device:TPU:24, one launch (start us, length us, event | category | flops | bytes accessed | tf_op | source)
XLA Modules:
  0.0 60.9 jit_solution(2703659100756051448)
XLA Ops:
  0.0 59.6 %relay_attention.1 = bf16[1,2,128,4096]{3,2,1,0:T(8,128)(2,1)S(1)} custom-call(s32[1,2,4]{2,1,0:T(2,128)} %lengths_ref.1, s32[1,2]{1,0:T(1,128)} %order_ref.1, bf16[1,2,128,4096]{3,2,1,0:T(8,128)(2,1)} %q_hbm.1, bf16[1,2,128,8,256]{4,3,2,1,0:T(8,128)(2,1)} %kv_hbm.1), custom_call_target="tpu_custom_call" | custom-call | tf_op jit(solution)/shard_map/relay_attention/pallas_call | solution.py:337
  59.6 1.3 %copy.6 = bf16[1,2,128,4096]{3,2,1,0:T(8,128)(2,1)} copy(bf16[1,2,128,4096]{3,2,1,0:T(8,128)(2,1)S(1)} %relay_attention.1) | data formatting | bytes 4194304

commit v6 on v5

--- a/solution.py
+++ b/solution.py
@@ -233,11 +233,11 @@
     q_copy.wait()
     factor = head**-0.5 * math.log2(math.e)
 
-    def compute(c):
+    def compute(c, turn_parts):
         j = c // groups
         k = kvbuf[c, :, :head]
         v = jnp.concatenate([kvbuf[c, :, head:], jnp.ones((keys, head), kvbuf.dtype)], axis=1)
-        for part in range(parts):
+        for part in turn_parts:
             first = pl.multiple_of((c % groups) * out_cols + part * part_cols, part_cols)
             q = qbuf[order_ref[0, j], :, pl.ds(first, part_cols)]
             stacked = jnp.concatenate(
@@ -275,13 +275,14 @@
                 def _(k=k):
                     arrived_and_on(t - (k - 1), k)
 
-        @pl.when(t >= hops)
-        def _():
-            c = t - hops
-            for d in range(1, reach + 1):
-                if d % width != 0:
-                    by_piece(c, d, lambda p, d=d: arrived(c, d, p))
-            compute(c)
+            @pl.when(t >= hops)
+            def _(k=k):
+                c = t - hops
+                if k == 1:
+                    for d in range(1, reach + 1):
+                        if d % width != 0:
+                            by_piece(c, d, lambda p, d=d: arrived(c, d, p))
+                compute(c, range((k - 1) * parts // hops, k * parts // hops))
 
         return carry
 

time: 61.6 us -> 61.6 us (level)
  no operation moved by 1% of the time
where the time goes in v6:
time: 61.6 us; the launch traced here: 60.9 us
  Pallas kernels  59.6 us (97%)
  local copies, waits for them, and re-layouts  1.32 us (2%)
    pallas_call x1, Pallas kernels, local(): pl.pallas_call(kernel, out_shape=jax.ShapeDtypeStruct(queries.shape, quer...  59.6 us
    unnamed x1, local copies, waits for them, and re-layouts  1.32 us

profile of v6, /device:TPU:24, one launch (start us, length us, event | category | flops | bytes accessed | tf_op | source)
XLA Modules:
  0.0 60.9 jit_solution(11617070644166179754)
XLA Ops:
  0.0 59.6 %relay_attention.1 = bf16[1,2,128,4096]{3,2,1,0:T(8,128)(2,1)S(1)} custom-call(s32[1,2,4]{2,1,0:T(2,128)} %lengths_ref.1, s32[1,2]{1,0:T(1,128)} %order_ref.1, bf16[1,2,128,4096]{3,2,1,0:T(8,128)(2,1)} %q_hbm.1, bf16[1,2,128,8,256]{4,3,2,1,0:T(8,128)(2,1)} %kv_hbm.1), custom_call_target="tpu_custom_call" | custom-call | tf_op jit(solution)/shard_map/relay_attention/pallas_call | solution.py:338
  59.6 1.3 %copy.6 = bf16[1,2,128,4096]{3,2,1,0:T(8,128)(2,1)} copy(bf16[1,2,128,4096]{3,2,1,0:T(8,128)(2,1)S(1)} %relay_attention.1) | data formatting | bytes 4194304

commit v7 on v6

--- a/solution.py
+++ b/solution.py
@@ -9,6 +9,7 @@
 
 MESH = pl.DeviceIdType.MESH
 LEAD = 3
+PERIOD = 8
 MASKED = -1e30
 
 
@@ -32,6 +33,7 @@
     recv_sem,
     column_sem,
     row_sem,
+    straight_sem,
     osend_sem,
     orecv_sem,
 ):
@@ -65,6 +67,16 @@
         if dx != 0 and 1 <= k * width + dx <= reach
     ]
 
+    straight = hops * width - 1
+    eased = row_moves.index((hops, -1)) if (hops, -1) in row_moves and straight > width else None
+    straight_count = chunks // PERIOD if eased is not None else 0
+
+    def goes_straight(c):
+        return c % PERIOD == PERIOD // 2 - 1
+
+    def straight_goes():
+        return (x + 1 < width) & (z + 1 < depth) & (z + 1 >= hops)
+
     def slot(c, d, p):
         rows = tok if p is None else tok // halves
         return kvbuf.at[c, pl.ds(d * tok + (p or 0) * rows, rows), :]
@@ -78,6 +90,16 @@
             dst_ref=slot(c, (k + 1) * width, p),
             send_sem=column_sem.at[k],
             recv_sem=arrival(c, (k + 1) * width, p),
+            device_id=(section, me + width),
+            device_id_type=MESH,
+        )
+
+    def straight_copy(c):
+        return pltpu.make_async_remote_copy(
+            src_ref=slot(c, straight - width, None),
+            dst_ref=slot(c, straight, None),
+            send_sem=straight_sem.at[0],
+            recv_sem=arrival(c, straight, None),
             device_id=(section, me + width),
             device_id_type=MESH,
         )
@@ -140,8 +162,18 @@
                     act(row_copy, index, k * width + dx)
 
     def start_sends(c, k, p=None):
+        def whole(copy, i, d):
+            if copy is row_copy and i == eased:
+
+                @pl.when(jnp.logical_not(goes_straight(c)))
+                def _():
+                    by_piece(c, d, lambda q: copy(c, i, q).start())
+
+            else:
+                by_piece(c, d, lambda q: copy(c, i, q).start())
+
         if p is None:
-            each_send(k, lambda copy, i, d: by_piece(c, d, lambda q: copy(c, i, q).start()))
+            each_send(k, whole)
         else:
             each_send(k, lambda copy, i, d: copy(c, i, p).start())
 
@@ -282,6 +314,12 @@
                     for d in range(1, reach + 1):
                         if d % width != 0:
                             by_piece(c, d, lambda p, d=d: arrived(c, d, p))
+                    if eased is not None:
+
+                        @pl.when(goes_straight(c) & straight_goes())
+                        def _():
+                            straight_copy(c).start()
+
                 compute(c, range((k - 1) * parts // hops, k * parts // hops))
 
         return carry
@@ -291,8 +329,8 @@
     def sent(ref, sem):
         pltpu.make_async_copy(ref, ref, sem).wait()
 
-    def drained(k):
-        return kvbuf.at[:, pl.ds(k * width * tok, tok), :]
+    def drained(k, count=chunks):
+        return kvbuf.at[pl.ds(0, count), pl.ds(k * width * tok, tok), :]
 
     for k in range(hops):
         if (k + 1) * width <= reach:
@@ -305,7 +343,13 @@
 
         @pl.when(row_goes(index))
         def _(k=k, index=index):
-            sent(drained(k), row_sem.at[index])
+            sent(drained(k, chunks - straight_count * (index == eased)), row_sem.at[index])
+
+    if eased is not None:
+
+        @pl.when(straight_goes())
+        def _():
+            sent(drained(0, straight_count), straight_sem.at[0])
 
     sent(obuf, osend_sem)
     sent(out_hbm.at[0], orecv_sem)
@@ -356,6 +400,7 @@
             pltpu.SemaphoreType.DMA((reach + 1, chunks + 1)),
             pltpu.SemaphoreType.DMA((hops,)),
             pltpu.SemaphoreType.DMA((max(1, moves),)),
+            pltpu.SemaphoreType.DMA((1,)),
             pltpu.SemaphoreType.DMA(()),
             pltpu.SemaphoreType.DMA(()),
         ],

time: 61.6 us -> 67 us (1.088)
  Pallas kernels: 59.6 us -> 64.9 us
    pallas_call x1, Pallas kernels: 59.6 us -> 64.9 us  [local(): pl.pallas_call(kernel, out_shape=jax.ShapeDtypeStruct(queries.shape, quer...]
where the time goes in v7:
time: 67 us; the launch traced here: 66.3 us
  Pallas kernels  64.9 us (97%)
  local copies, waits for them, and re-layouts  1.32 us (2%)
    pallas_call x1, Pallas kernels, local(): pl.pallas_call(kernel, out_shape=jax.ShapeDtypeStruct(queries.shape, quer...  64.9 us

profile of v7, /device:TPU:24, one launch (start us, length us, event | category | flops | bytes accessed | tf_op | source)
XLA Modules:
  0.0 66.3 jit_solution(10535126826584891403)
XLA Ops:
  0.0 64.9 %relay_attention.1 = bf16[1,2,128,4096]{3,2,1,0:T(8,128)(2,1)S(1)} custom-call(s32[1,2,4]{2,1,0:T(2,128)} %lengths_ref.1, s32[1,2]{1,0:T(1,128)} %order_ref.1, bf16[1,2,128,4096]{3,2,1,0:T(8,128)(2,1)} %q_hbm.1, bf16[1,2,128,8,256]{4,3,2,1,0:T(8,128)(2,1)} %kv_hbm.1), custom_call_target="tpu_custom_call" | custom-call | tf_op jit(solution)/shard_map/relay_attention/pallas_call | solution.py:382
  64.9 1.3 %copy.6 = bf16[1,2,128,4096]{3,2,1,0:T(8,128)(2,1)} copy(bf16[1,2,128,4096]{3,2,1,0:T(8,128)(2,1)S(1)} %relay_attention.1) | data formatting | bytes 4194304

commit v8 on v6

--- a/solution.py
+++ b/solution.py
@@ -9,6 +9,7 @@
 
 MESH = pl.DeviceIdType.MESH
 LEAD = 3
+LAG = 1
 MASKED = -1e30
 
 
@@ -275,9 +276,9 @@
                 def _(k=k):
                     arrived_and_on(t - (k - 1), k)
 
-            @pl.when(t >= hops)
+            @pl.when(t >= hops + LAG)
             def _(k=k):
-                c = t - hops
+                c = t - hops - LAG
                 if k == 1:
                     for d in range(1, reach + 1):
                         if d % width != 0:
@@ -286,7 +287,7 @@
 
         return carry
 
-    lax.fori_loop(0, chunks + hops, turn, 0)
+    lax.fori_loop(0, chunks + hops + LAG, turn, 0)
 
     def sent(ref, sem):
         pltpu.make_async_copy(ref, ref, sem).wait()

time: 61.6 us -> 61.1 us (level)
  no operation moved by 1% of the time
where the time goes in v8:
time: 61.1 us; the launch traced here: 60.6 us
  Pallas kernels  59.3 us (97%)
  local copies, waits for them, and re-layouts  1.32 us (2%)
    pallas_call x1, Pallas kernels, local(): pl.pallas_call(kernel, out_shape=jax.ShapeDtypeStruct(queries.shape, quer...  59.3 us
    unnamed x1, local copies, waits for them, and re-layouts  1.32 us

profile of v8, /device:TPU:24, one launch (start us, length us, event | category | flops | bytes accessed | tf_op | source)
XLA Modules:
  0.0 60.6 jit_solution(16244190681316803630)
XLA Ops:
  0.0 59.3 %relay_attention.1 = bf16[1,2,128,4096]{3,2,1,0:T(8,128)(2,1)S(1)} custom-call(s32[1,2,4]{2,1,0:T(2,128)} %lengths_ref.1, s32[1,2]{1,0:T(1,128)} %order_ref.1, bf16[1,2,128,4096]{3,2,1,0:T(8,128)(2,1)} %q_hbm.1, bf16[1,2,128,8,256]{4,3,2,1,0:T(8,128)(2,1)} %kv_hbm.1), custom_call_target="tpu_custom_call" | custom-call | tf_op jit(solution)/shard_map/relay_attention/pallas_call | solution.py:339
  59.3 1.3 %copy.6 = bf16[1,2,128,4096]{3,2,1,0:T(8,128)(2,1)} copy(bf16[1,2,128,4096]{3,2,1,0:T(8,128)(2,1)S(1)} %relay_attention.1) | data formatting | bytes 4194304

commit v9 on v8

--- a/solution.py
+++ b/solution.py
@@ -8,7 +8,7 @@
 from jax.sharding import PartitionSpec as P
 
 MESH = pl.DeviceIdType.MESH
-LEAD = 3
+LEAD = 1
 LAG = 1
 MASKED = -1e30
 
@@ -194,7 +194,7 @@
                 ].astype(kvbuf.dtype)
             then(g)
 
-    leads = [min(LEAD, groups), min(2, groups), 1]
+    leads = [min(LEAD, groups), min(2, LEAD), 1]
     turns = [0, chunks // 2, chunks * 3 // 4, chunks]
 
     def first_sends(g):

time: 61.1 us -> 58.9 us (0.964)
  Pallas kernels: 59.3 us -> 56.8 us
    pallas_call x1, Pallas kernels: 59.3 us -> 56.8 us  [local(): pl.pallas_call(kernel, out_shape=jax.ShapeDtypeStruct(queries.shape, quer...]
where the time goes in v9:
time: 58.9 us; the launch traced here: 58.1 us
  Pallas kernels  56.8 us (96%)
  local copies, waits for them, and re-layouts  1.32 us (2%)
    pallas_call x1, Pallas kernels, local(): pl.pallas_call(kernel, out_shape=jax.ShapeDtypeStruct(queries.shape, quer...  56.8 us
    unnamed x1, local copies, waits for them, and re-layouts  1.32 us

profile of v9, /device:TPU:24, one launch (start us, length us, event | category | flops | bytes accessed | tf_op | source)
XLA Modules:
  0.0 58.1 jit_solution(9731823117403884544)
XLA Ops:
  0.0 56.8 %relay_attention.1 = bf16[1,2,128,4096]{3,2,1,0:T(8,128)(2,1)S(1)} custom-call(s32[1,2,4]{2,1,0:T(2,128)} %lengths_ref.1, s32[1,2]{1,0:T(1,128)} %order_ref.1, bf16[1,2,128,4096]{3,2,1,0:T(8,128)(2,1)} %q_hbm.1, bf16[1,2,128,8,256]{4,3,2,1,0:T(8,128)(2,1)} %kv_hbm.1), custom_call_target="tpu_custom_call" | custom-call | tf_op jit(solution)/shard_map/relay_attention/pallas_call | solution.py:339
  56.8 1.3 %copy.6 = bf16[1,2,128,4096]{3,2,1,0:T(8,128)(2,1)} copy(bf16[1,2,128,4096]{3,2,1,0:T(8,128)(2,1)S(1)} %relay_attention.1) | data formatting | bytes 4194304

commit v10 on v9

--- a/solution.py
+++ b/solution.py
@@ -71,7 +71,7 @@
         return kvbuf.at[c, pl.ds(d * tok + (p or 0) * rows, rows), :]
 
     def arrival(c, d, p):
-        return recv_sem.at[d, chunks if p == 1 else c]
+        return recv_sem.at[d, chunks + jnp.where(c == 0, 1, 0) if p == 1 else c]
 
     def column_copy(c, k, p):
         return pltpu.make_async_remote_copy(
@@ -106,15 +106,15 @@
         )
 
     def by_piece(c, d, act):
-        if d <= (hops - 1) * width:
-            act(None)
-            return
-
-        @pl.when(c < last)
+        cut = c == 0
+        if d > (hops - 1) * width:
+            cut = cut | (c == last)
+
+        @pl.when(jnp.logical_not(cut))
         def _():
             act(None)
 
-        @pl.when(c == last)
+        @pl.when(cut)
         def _():
             for p in range(halves):
                 act(p)
@@ -354,7 +354,7 @@
             pltpu.VMEM((chunks, share // joint, tok, joint * head), jnp.bfloat16),
             pltpu.VMEM((micro, tok, keys), jnp.float32),
             pltpu.SemaphoreType.DMA((1 + micro,)),
-            pltpu.SemaphoreType.DMA((reach + 1, chunks + 1)),
+            pltpu.SemaphoreType.DMA((reach + 1, chunks + 2)),
             pltpu.SemaphoreType.DMA((hops,)),
             pltpu.SemaphoreType.DMA((max(1, moves),)),
             pltpu.SemaphoreType.DMA(()),

time: 58.9 us -> 58.9 us (level)
  no operation moved by 1% of the time
where the time goes in v10:
time: 58.9 us; the launch traced here: 58.2 us
  Pallas kernels  56.9 us (97%)
  local copies, waits for them, and re-layouts  1.32 us (2%)
    pallas_call x1, Pallas kernels, local(): pl.pallas_call(kernel, out_shape=jax.ShapeDtypeStruct(queries.shape, quer...  56.9 us
    unnamed x1, local copies, waits for them, and re-layouts  1.32 us

profile of v10, /device:TPU:24, one launch (start us, length us, event | category | flops | bytes accessed | tf_op | source)
XLA Modules:
  0.0 58.2 jit_solution(7729243664305400379)
XLA Ops:
  0.0 56.9 %relay_attention.1 = bf16[1,2,128,4096]{3,2,1,0:T(8,128)(2,1)S(1)} custom-call(s32[1,2,4]{2,1,0:T(2,128)} %lengths_ref.1, s32[1,2]{1,0:T(1,128)} %order_ref.1, bf16[1,2,128,4096]{3,2,1,0:T(8,128)(2,1)} %q_hbm.1, bf16[1,2,128,8,256]{4,3,2,1,0:T(8,128)(2,1)} %kv_hbm.1), custom_call_target="tpu_custom_call" | custom-call | tf_op jit(solution)/shard_map/relay_attention/pallas_call | solution.py:339
  56.9 1.3 %copy.6 = bf16[1,2,128,4096]{3,2,1,0:T(8,128)(2,1)} copy(bf16[1,2,128,4096]{3,2,1,0:T(8,128)(2,1)S(1)} %relay_attention.1) | data formatting | bytes 4194304
